TPU v7x, 128 devices: a whole 4x4x4 slice. The times are simulated.
128 devices in a mesh: grp: 16 (over y, z), tp: 8 (over x, core).
Axes of the slice: x: 4, y: 4, z: 4, core: 2. Of those that a mesh axis runs over, the one named last changes fastest.
Arguments:
- queries: bfloat16 [2, 512, 128, 576], P(None, 'grp', 'tp'), may hold values from -48 to 48
- new_latent: bfloat16 [2, 512, 576], P(None, 'grp'), may hold values from -7 to 7
- latent_cache: bfloat16 [327680, 576], P('grp'), may hold values from -8 to 8
- tables: int32 [512, 10], P('grp'), may hold values from 0 to 319, as said below
- context_len: int32 [256], replicated, may hold values from 213 to 640, as said below
- group_rows: int32 [16], replicated, may hold values from 1 to 32, 256 in all
- request_order: int32 [256], replicated, may hold values from 0 to 255, each once
- residual: bfloat16 [2, 256, 7168], P(None, None, 'grp'), may hold values from -24 to 24
- value_up: bfloat16 [128, 512, 128], P('tp'), may hold values from -4 to 4
- out_proj: bfloat16 [16384, 7168], P('tp', 'grp'), may hold values from -0.046875 to 0.046875
- norm_gain: bfloat16 [7168], P('grp'), may hold values from 0.099609375 to 1.8984375
- gate_proj: bfloat16 [7168, 18432], P('grp', 'tp'), may hold values from -0.0625 to 0.0625
- up_proj: bfloat16 [7168, 18432], P('grp', 'tp'), may hold values from -0.0625 to 0.0625
- down_proj: bfloat16 [18432, 7168], P('tp', 'grp'), may hold values from -0.046875 to 0.046875
Outputs:
- layer_out: bfloat16 [2, 256, 7168], P(None, 'tp', 'grp')
Inputs may be any that keep to these rules, and one draw needn't show every extreme that they name: `tables`: within each group all block ids of its 32 slots are distinct; a context fills its slot's blocks from the first on. `context_len`: one request has a context of exactly 640. `group_rows`: sums to 256; some group has exactly 32 requests; the live requests of group g sit in its first group_rows[g] slots. `request_order`: each position is taken by exactly one request.
All inputs are finite; a program needn't handle non-finite values.
Results may differ from a plain program's by a relative error of at most 0.009.
Values may be sent and summed in bfloat16 or wider, within the bound.
A program may use at most 192 MiB of HBM per device.

v0:
```python
import jax
import jax.numpy as jnp
from jax import lax
from jax.sharding import PartitionSpec as P

D = 7168


score_scale = 192.0 ** (-0.5)


def slot_positions(group_rows, request_order, slot_count):
    group_ends = jnp.cumsum(group_rows)
    group_starts = group_ends - group_rows
    group_of = jnp.sum((request_order[:, None] >= group_ends[None, :]).astype(jnp.int32), axis=1)
    in_group = group_of[:, None] == jnp.arange(group_rows.shape[0], dtype=jnp.int32)[None, :]
    first_slot = jnp.sum(jnp.where(in_group, group_starts[None, :], 0), axis=1)
    return group_of * slot_count + request_order - first_slot


def shards(
    queries,
    new_latent,
    latent_cache,
    tables,
    context_len,
    group_rows,
    request_order,
    residual,
    value_up,
    out_proj,
    norm_gain,
    gate_proj,
    up_proj,
    down_proj,
):
    slot_count, block_count = tables.shape
    block_size = latent_cache.shape[0] // (slot_count * block_count)
    latent_rank = value_up.shape[1]
    requests = request_order.shape[0]
    tp_count = lax.axis_size("tp")
    my_requests = requests // tp_count
    group_index = lax.axis_index("grp")
    slot_index = slot_positions(group_rows, request_order, slot_count)
    my_slots = group_index * slot_count + jnp.arange(slot_count, dtype=jnp.int32)
    matches = slot_index[None, :] == my_slots[:, None]
    slot_len = jnp.sum(jnp.where(matches, context_len[None, :], 0), axis=1)
    pool_blocks = latent_cache.reshape(-1, block_size, latent_cache.shape[1])
    key_rows = jnp.take(pool_blocks, tables, axis=0).reshape(
        slot_count, block_count * block_size, latent_cache.shape[1]
    )
    span = key_rows.shape[1]
    cached = (
        jnp.einsum("pshk,stk->psht", queries, key_rows, preferred_element_type=jnp.float32)
        * score_scale
    )
    live = jnp.arange(span, dtype=jnp.int32)[None, :] < slot_len[:, None]
    cached = jnp.where(live[None, :, None, :], cached, -jnp.inf)
    current = (
        jnp.einsum("pshk,nsk->pshn", queries, new_latent, preferred_element_type=jnp.float32)
        * score_scale
    )
    visible = jnp.arange(2, dtype=jnp.int32)[None, :] <= jnp.arange(2, dtype=jnp.int32)[:, None]
    current = jnp.where(visible[:, None, None, :], current, -jnp.inf)
    scores = jnp.concatenate([cached, current], axis=3)
    largest = jnp.max(scores, axis=3, keepdims=True)
    expo = jnp.exp(scores - largest)
    weights = (expo / jnp.sum(expo, axis=3, keepdims=True)).astype(jnp.bfloat16)
    mixed = jnp.einsum(
        "psht,str->pshr", weights[..., :span], key_rows, preferred_element_type=jnp.float32
    )[..., :latent_rank]
    mixed = (
        mixed
        + jnp.einsum(
            "pshn,nsr->pshr", weights[..., span:], new_latent, preferred_element_type=jnp.float32
        )[..., :latent_rank]
    )
    latent_out = mixed.astype(jnp.bfloat16)
    heads_out = jnp.einsum(
        "pshr,hrv->pshv", latent_out, value_up, preferred_element_type=jnp.float32
    ).astype(jnp.bfloat16)
    heads_out = heads_out.reshape(heads_out.shape[0], slot_count, -1)

    def project(portion):
        return jnp.einsum("psv,vd->psd", portion, out_proj, preferred_element_type=jnp.float32)

    def finish(head_block, residual_block):
        step_count = head_block.shape[0]
        partials = project(lax.all_gather(head_block, "grp", axis=1, tiled=True))
        partials = jnp.take(partials, slot_index, axis=1)
        attention = lax.psum(partials, "tp")
        stream = residual_block.astype(jnp.float32) + attention
        squares = lax.psum(jnp.sum(stream * stream, axis=2), "grp")
        inverse_rms = lax.rsqrt(squares / D + 1e-06)
        normed = (stream * inverse_rms[..., None] * norm_gain.astype(jnp.float32)).astype(
            jnp.bfloat16
        )
        normed = jnp.swapaxes(normed, 0, 1).reshape(requests * step_count, -1)
        gate_local = jnp.dot(normed, gate_proj, preferred_element_type=jnp.float32)
        up_local = jnp.dot(normed, up_proj, preferred_element_type=jnp.float32)
        gate_part, up_part = lax.psum((gate_local, up_local), "grp")
        hidden = (jax.nn.silu(gate_part) * up_part).astype(jnp.bfloat16)
        reduced = lax.psum_scatter(
            jnp.dot(hidden, down_proj, preferred_element_type=jnp.float32).astype(jnp.bfloat16),
            "tp",
            scatter_dimension=0,
            tiled=True,
        ).astype(jnp.float32)
        reduced = jnp.swapaxes(reduced.reshape(my_requests, step_count, -1), 0, 1)
        mine = lax.dynamic_slice_in_dim(stream, lax.axis_index("tp") * my_requests, my_requests, 1)
        return (mine + reduced).astype(jnp.bfloat16)

    layer_out = jnp.concatenate(
        [
            finish(heads_out[step_index : step_index + 1], residual[step_index : step_index + 1])
            for step_index in range(2)
        ],
        axis=0,
    )
    return layer_out


def solution(mesh):
    placed = (
        P(None, "grp", "tp", None),
        P(None, "grp", None),
        P("grp", None),
        P("grp", None),
        P(),
        P(),
        P(),
        P(None, None, "grp"),
        P("tp", None, None),
        P("tp", "grp"),
        P("grp"),
        P("grp", "tp"),
        P("grp", "tp"),
        P("tp", "grp"),
    )
    return jax.shard_map(
        shards, mesh=mesh, in_specs=placed, out_specs=P(None, "tp", "grp"), check_vma=False
    )
```

profile of v0, /device:TPU:1, one launch (start us, length us, event | category | flops | bytes accessed | tf_op | source)
XLA Modules:
  0.0 561.9 jit_solution(1650699125969779665)
XLA Ops:
  6.5 0.8 compare_select_fusion
  11.2 0.9 select_reduce_fusion
  12.2 31.1 %copy.103 = bf16[20480,576]{1,0:T(8,128)(2,1)} copy(bf16[20480,576]{0,1:T(8,128)(2,1)} %param.18) | data formatting | bytes 47185920 | tf_op args[2]
  43.9 3.2 fusion.25
  47.9 22.1 %gather_fusion = bf16[320,64,576]{2,1,0:T(8,128)(2,1)} fusion(bf16[320,64,576]{2,1,0:T(8,128)(2,1)} %bitcast.89, s32[1024]{0:T(1024)S(1)} %pad_clamp_fusion.1), kind=kCustom, calls=%fused_computation.2 | custom fusion | bytes 47187200 | tf_op jit(solution)/shard_map/jit(_take)/gather | solution.py:49
  70.0 22.8 %bitcast_select_fusion = bf16[32,640,576]{2,1,0:T(8,128)(2,1)} fusion(pred[32,640]{1,0:T(8,128)(4,1)S(1)} %broadcast_in_dim.94, bf16[32,640,576]{2,1,0:T(8,128)(2,1)} %bitcast.90), kind=kLoop, calls=%fused_computation.7 | loop fusion | flops 11796480 | bytes 47206400 | tf_op jit(solution)/shard_map/jit(_take)/select_n | solution.py:49
  92.7 14.0 %fusion.48 = (f32[2,32,16]{2,0,1:T(2,128)S(1)}, f32[2,32,16,640]{3,2,0,1:T(8,128)}) fusion(bf16[2,32,16,576]{3,2,1,0:T(8,128)(2,1)} %param.16, bf16[32,640,576]{2,1,0:T(8,128)(2,1)} %bitcast_select_fusion, pred[32,640]{1,0:T(8,128)(4,1)S(1)} %iota_compare_fusion), kind=kOutput, calls=%fused_computation.81 | convolution fusion | flops 756939776 | bytes 27418624 | tf_op jit(solution)/shard_map/pshk,stk->psht/dot_general | solution.py:54
  106.8 2.6 fusion.5
  109.4 1.7 divide_convert_fusion
  111.1 12.3 %fusion.13 = f32[2,32,16,576]{3,2,0,1:T(8,128)} fusion(bf16[32,640,576]{2,1,0:T(8,128)(2,1)} %bitcast_select_fusion, bf16[2,32,16,642]{3,2,0,1:T(8,128)(2,1)} %divide_convert_fusion), kind=kOutput, calls=%fused_computation.24 | convolution fusion | flops 754974720 | bytes 29884416 | tf_op jit(solution)/shard_map/psht,str->pshr/dot_general | solution.py:69
  123.3 1.6 convolution_bitcast_fusion
  125.6 1.4 fusion.22
  128.7 46.6 %all-gather.5.cloned.1.call-done = bf16[1,512,2048]{2,1,0:T(8,128)(2,1)} async-done(((bf16[1,32,2048]{2,1,0:T(8,128)(2,1)}), bf16[1,512,2048]{2,1,0:T(8,128)(2,1)}) %all-gather.5.cloned.1.call-update) | async-done | bytes 2097168 | tf_op jit(solution)/shard_map/all_gather | solution.py:89
  175.3 3.4 fusion.9
  178.7 1.8 gather_fusion.2
  180.5 41.5 %all-gather.3.cloned.1.call-done = bf16[1,512,2048]{2,1,0:T(8,128)(2,1)} async-done(((bf16[1,32,2048]{2,1,0:T(8,128)(2,1)}), bf16[1,512,2048]{2,1,0:T(8,128)(2,1)}) %all-gather.3.cloned.1.call-update) | async-done | bytes 2097168 | tf_op jit(solution)/shard_map/all_gather | solution.py:89
  222.0 3.4 fusion.11
  225.4 1.8 gather_fusion.1
  227.2 2.4 bitcast_select_fusion.2
  229.9 0.8 copy.136
  230.7 59.9 %all-reduce.8.cloned.1.call-done = (f32[1,256,448]{2,1,0:T(8,128)}, f32[1,256,448]{2,1,0:T(8,128)}) async-done(((f32[1,256,448]{2,1,0:T(8,128)}, f32[1,256,448]{2,1,0:T(8,128)}), (f32[1,256,448]{2,1,0:T(8,128)}, f32[1,256,448]{2,1,0:T(8,128)})) %all-reduce.8.cloned.1.call-update) | async-done | bytes 917520 | tf_op jit(solution)/shard_map/psum | solution.py:91
  290.6 1.5 multiply_reduce_fusion
  292.1 33.5 %all-reduce = (f32[1,256]{1,0:T(1,128)S(1)}, f32[1,256]{1,0:T(1,128)S(1)}) all-reduce(f32[1,256]{1,0:T(1,128)S(1)} %bitcast.99, f32[1,256]{1,0:T(1,128)S(1)} %bitcast.100), channel_id=1, replica_groups=mesh['grp'=16,'tp'=8] {'grp'}, use_global_device_ids=true, to_apply=%region_15.17 | all-reduce | flops 512 | bytes 4096 | tf_op jit(solution)/shard_map/psum | solution.py:93
  325.6 4.0 fusion.44
  329.5 2.2 fusion.42
  331.8 2.3 fusion.40
  334.1 2.2 fusion.38
  336.4 153.7 %all-reduce.6.cloned.1.call-done = (f32[256,2304]{1,0:T(8,128)}, f32[256,2304]{1,0:T(8,128)}, f32[256,2304]{1,0:T(8,128)}, f32[256,2304]{1,0:T(8,128)}) async-done(((f32[256,2304]{1,0:T(8,128)}, f32[256,2304]{1,0:T(8,128)}, f32[256,2304]{1,0:T(8,128)}, f32[256,2304]{1,0:T(8,128)}), (f32[256,2304]{1,0:T(8,128)}, f32[256,2304]{1,0:T(8,128)}, f32[256,2304]{1,0:T(8,128)}, ...) | async-done | bytes 9437200 | tf_op jit(solution)/shard_map/psum | solution.py:101
  490.2 4.5 convolution_convert_fusion.1
  494.7 4.5 convolution_convert_fusion
  499.3 22.8 %reduce-scatter.3.cloned.1.call-done = bf16[32,448]{1,0:T(8,128)(2,1)} async-done(((bf16[256,448]{1,0:T(8,128)(2,1)}), bf16[32,448]{1,0:T(8,128)(2,1)}) %reduce-scatter.3.cloned.1.call-update) | async-done | bytes 28688 | tf_op jit(solution)/shard_map/reduce_scatter | solution.py:103
  522.9 30.8 %reduce-scatter.5.cloned.1.call-done = bf16[32,448]{1,0:T(8,128)(2,1)} async-done(((bf16[256,448]{1,0:T(8,128)(2,1)}), bf16[32,448]{1,0:T(8,128)(2,1)}) %reduce-scatter.5.cloned.1.call-update) | async-done | bytes 28688 | tf_op jit(solution)/shard_map/reduce_scatter | solution.py:103
  (64 shorter events, 10.3 us)
Async XLA Ops:
  6.5 119.1 %copy-start = (bf16[16,512,128]{2,1,0:T(8,128)(2,1)S(1)}, bf16[16,512,128]{2,1,0:T(8,128)(2,1)}, u32[]{:S(2)}) copy-start(bf16[16,512,128]{2,1,0:T(8,128)(2,1)} %param.24) | copy-start | bytes 6291460
  6.5 168.8 %all-gather.5.cloned.1.call-start = ((), (), s32[]{:S(2)}) async-start(), calls=%async_computation.4 | async-start | bytes 2228224 | tf_op jit(solution)/shard_map/all_gather | solution.py:89
  12.1 31.7 %copy-start.6 = (bf16[2,32,576]{2,1,0:T(8,128)(2,1)S(1)}, bf16[2,32,576]{2,1,0:T(8,128)(2,1)}, u32[]{:S(2)}) copy-start(bf16[2,32,576]{2,1,0:T(8,128)(2,1)} %param.17) | copy-start | bytes 221188
  106.7 2.7 copy-start.2
  123.3 1.8 copy-start.1
  127.7 94.3 %all-gather.3.cloned.1.call-start = ((), (), s32[]{:S(2)}) async-start(), calls=%async_computation.2 | async-start | bytes 2228224 | tf_op jit(solution)/shard_map/all_gather | solution.py:89
  128.5 162.1 %all-reduce.8.cloned.1.call-start = ((), (), s32[]{:S(2)}) async-start(), calls=%async_computation.7 | async-start | bytes 2097152 | tf_op jit(solution)/shard_map/psum | solution.py:91
  227.2 2.5 copy-start.5
  227.2 3.5 copy-start.7
  229.6 260.5 %all-reduce.6.cloned.1.call-start = ((), (), s32[]{:S(2)}) async-start(), calls=%async_computation.6 | async-start | bytes 18874368 | tf_op jit(solution)/shard_map/psum | solution.py:101
  325.5 4.0 copy-start.4
  329.5 2.2 copy-start.3
  336.4 185.8 %reduce-scatter.3.cloned.1.call-start = ((), (), s32[]{:S(2)}) async-start(), calls=%async_computation.3 | async-start | bytes 294912 | tf_op jit(solution)/shard_map/reduce_scatter | solution.py:103
  494.7 59.0 %reduce-scatter.5.cloned.1.call-start = ((), (), s32[]{:S(2)}) async-start(), calls=%async_computation.5 | async-start | bytes 294912 | tf_op jit(solution)/shard_map/reduce_scatter | solution.py:103
Sparse Core Ops, SparseCore 0:
  127.8 47.4 all-gather.4
  177.5 44.5 all-gather.2
  229.7 60.7 all-reduce.7
  336.5 153.6 all-reduce.5
  494.8 27.2 reduce-scatter.2
  524.3 29.3 reduce-scatter.4
where the time goes:
time: 565 us; the launch traced here: 562 us
  waiting for transfers between devices  355 us (63%)
  local copies, waits for them, and re-layouts  61.4 us (11%)
  matrix products  59.1 us (10%)
  other arithmetic  38.5 us (7%)
  blocking collectives  33.5 us (6%)
  between operations  13.7 us (2%)
    psum x1, waiting for transfers between devices, finish(): gate_part, up_part = lax.psum((gate_local, up_local), 'grp')  154 us
    all_gather x2, waiting for transfers between devices, finish(): partials = project(lax.all_gather(head_block, 'grp', axis=1, tiled=True))  88.1 us
    psum x1, waiting for transfers between devices, finish(): attention = lax.psum(partials, 'tp')  59.9 us
    reduce_scatter x2, waiting for transfers between devices, finish(): lax.psum_scatter(jnp.dot(hidden, down_proj, preferred_element_type=jnp.fl...  53.6 us
    psum x1, blocking collectives, finish(): squares = lax.psum(jnp.sum(stream * stream, axis=2), 'grp')  33.5 us
    unnamed x20, local copies, waits for them, and re-layouts  32.4 us
    select_n x2, other arithmetic, shards(): jnp.take(pool_blocks, tables, axis=0)  23.6 us
    gather x1, local copies, waits for them, and re-layouts, shards(): jnp.take(pool_blocks, tables, axis=0)  22.1 us
  transfers between devices with their start and end apart: 6, of which 6 were waited for; matrix products, arithmetic and copies ran while one was open for 2% of the time, Pallas kernels for 0%

commit v1 on v0

--- a/solution.py
+++ b/solution.py
@@ -1,12 +1,156 @@
+import functools
+
 import jax
 import jax.numpy as jnp
 from jax import lax
+from jax.experimental import pallas as pl
+from jax.experimental.pallas import tpu as pltpu
 from jax.sharding import PartitionSpec as P
 
 D = 7168
-
+SLOTS = 32
+BLOCKS = 10
+BLOCK = 64
+SPAN = BLOCKS * BLOCK
+HEADS = 16
+KDIM = 576
+RANK = 512
+VH = 128
+GRPS = 16
+REQS = 256
 
 score_scale = 192.0 ** (-0.5)
+NT = (((1,), (1,)), ((), ()))
+
+
+def attention_kernel(
+    tables, order, ctx, rows, q_ref, new_ref, cache, vup_ref, out_ref, raw, keys, lat, fresh_all, lens, sems
+):
+    group = lax.axis_index("grp")
+
+    def add_rows(j, total):
+        return total + jnp.where(j < group, rows[j], 0)
+
+    start = lax.fori_loop(0, GRPS, add_rows, 0)
+    live = rows[group]
+
+    def clear(i, carry):
+        lens[i] = 0
+        return carry
+
+    lax.fori_loop(0, SLOTS + 1, clear, 0)
+
+    def put_len(r, carry):
+        where = order[r] - start
+        inside = jnp.logical_and(where >= 0, where < live)
+        lens[jnp.where(inside, where, SLOTS)] = ctx[r]
+        return carry
+
+    lax.fori_loop(0, REQS, put_len, 0, unroll=8)
+
+    def copies(pair, buf, action):
+        for k in range(2):
+            slot = pair * 2 + k
+            count = jnp.where(slot < live, (lens[slot] + BLOCK - 1) // BLOCK, 0)
+            for j in range(BLOCKS):
+
+                @pl.when(j < count)
+                def _():
+                    block = tables[slot * BLOCKS + j]
+                    first = pl.multiple_of((block // 2) * (2 * BLOCK), 2 * BLOCK)
+                    action(
+                        pltpu.make_async_copy(
+                            cache.at[:, pl.ds(first, 2 * BLOCK)],
+                            raw.at[buf, k * BLOCKS + j],
+                            sems.at[buf, k * BLOCKS + j],
+                        )
+                    )
+
+    pairs = (live + 1) // 2
+    raw[...] = jnp.zeros_like(raw)
+    copies(0, 0, lambda c: c.start())
+    lat[...] = jnp.zeros_like(lat)
+    fresh_all[...] = new_ref[...].astype(jnp.float32)
+    low = lax.broadcasted_iota(jnp.int32, (KDIM, 2 * BLOCK), 1) < BLOCK
+    position = lax.broadcasted_iota(jnp.int32, (2 * HEADS, SPAN), 1)
+    step_of = lax.broadcasted_iota(jnp.int32, (2 * HEADS, 1), 0) // HEADS
+
+    def one_pair(pair, carry):
+        buf = lax.rem(pair, 2)
+        copies(pair, buf, lambda c: c.wait())
+
+        @pl.when(pair + 1 < pairs)
+        def _():
+            copies(pair + 1, 1 - buf, lambda c: c.start())
+
+        for k in range(2):
+            slot = pair * 2 + k
+            for j in range(BLOCKS // 2):
+                odd_a = lax.rem(tables[slot * BLOCKS + 2 * j], 2)
+                odd_b = lax.rem(tables[slot * BLOCKS + 2 * j + 1], 2)
+                a = raw[buf, k * BLOCKS + 2 * j]
+                b = raw[buf, k * BLOCKS + 2 * j + 1]
+                a = pltpu.roll(a, odd_a * BLOCK, 1)
+                b = pltpu.roll(b, (1 - odd_b) * BLOCK, 1)
+                keys[k, :, j * 128 : (j + 1) * 128] = jnp.where(low, a, b)
+        for k in range(2):
+            slot = pair * 2 + k
+            q = q_ref[:, slot].reshape(2 * HEADS, KDIM)
+            fresh_float = [fresh_all[t, pl.ds(slot, 1), :] for t in range(2)]
+            scores = jnp.dot(q, keys[k], preferred_element_type=jnp.float32) * score_scale
+            scores = jnp.where(position < lens[slot], scores, -jnp.inf)
+            q_float = q.astype(jnp.float32)
+            now = jnp.sum(q_float * fresh_float[0], axis=1, keepdims=True) * score_scale
+            later = jnp.sum(q_float * fresh_float[1], axis=1, keepdims=True) * score_scale
+            later = jnp.where(step_of == 1, later, -jnp.inf)
+            largest = jnp.maximum(jnp.max(scores, axis=1, keepdims=True), jnp.maximum(now, later))
+            expo = jnp.exp(scores - largest)
+            now = jnp.exp(now - largest)
+            later = jnp.exp(later - largest)
+            inverse = 1.0 / (jnp.sum(expo, axis=1, keepdims=True) + now + later)
+            mixed = lax.dot_general(
+                expo.astype(jnp.bfloat16), keys[k, :RANK, :], NT, preferred_element_type=jnp.float32
+            )
+            mixed = mixed + now * fresh_float[0][:, :RANK] + later * fresh_float[1][:, :RANK]
+            lat[slot] = mixed * inverse
+        return carry
+
+    lax.fori_loop(0, pairs, one_pair, 0)
+
+    for h in range(HEADS):
+        both = jnp.concatenate([lat[:, h, :], lat[:, HEADS + h, :]], axis=0).astype(jnp.bfloat16)
+        value = jnp.dot(both, vup_ref[h], preferred_element_type=jnp.float32).astype(jnp.bfloat16)
+        out_ref[0, :, h * VH : (h + 1) * VH] = value[:SLOTS]
+        out_ref[1, :, h * VH : (h + 1) * VH] = value[SLOTS:]
+
+
+def attend(queries, new_latent, latent_cache, tables, context_len, group_rows, request_order, value_up):
+    smem = pl.BlockSpec(memory_space=pltpu.SMEM)
+    vmem = pl.BlockSpec(memory_space=pltpu.VMEM)
+    return pl.pallas_call(
+        attention_kernel,
+        out_shape=jax.ShapeDtypeStruct((2, SLOTS, HEADS * VH), jnp.bfloat16),
+        in_specs=[smem] * 4 + [vmem, vmem, pl.BlockSpec(memory_space=pl.ANY), vmem],
+        out_specs=vmem,
+        scratch_shapes=[
+            pltpu.VMEM((2, 2 * BLOCKS, KDIM, 2 * BLOCK), jnp.bfloat16),
+            pltpu.VMEM((2, KDIM, SPAN), jnp.bfloat16),
+            pltpu.VMEM((SLOTS, 2 * HEADS, RANK), jnp.float32),
+            pltpu.VMEM((2, SLOTS, KDIM), jnp.float32),
+            pltpu.SMEM((SLOTS + 1,), jnp.int32),
+            pltpu.SemaphoreType.DMA((2, 2 * BLOCKS)),
+        ],
+        compiler_params=pltpu.CompilerParams(vmem_limit_bytes=40 << 20),
+    )(
+        tables.reshape(-1),
+        request_order,
+        context_len,
+        group_rows,
+        queries,
+        new_latent,
+        latent_cache.T,
+        value_up,
+    )
 
 
 def slot_positions(group_rows, request_order, slot_count):
@@ -34,52 +178,14 @@
     up_proj,
     down_proj,
 ):
-    slot_count, block_count = tables.shape
-    block_size = latent_cache.shape[0] // (slot_count * block_count)
-    latent_rank = value_up.shape[1]
+    slot_count = tables.shape[0]
     requests = request_order.shape[0]
     tp_count = lax.axis_size("tp")
     my_requests = requests // tp_count
-    group_index = lax.axis_index("grp")
+    heads_out = attend(
+        queries, new_latent, latent_cache, tables, context_len, group_rows, request_order, value_up
+    )
     slot_index = slot_positions(group_rows, request_order, slot_count)
-    my_slots = group_index * slot_count + jnp.arange(slot_count, dtype=jnp.int32)
-    matches = slot_index[None, :] == my_slots[:, None]
-    slot_len = jnp.sum(jnp.where(matches, context_len[None, :], 0), axis=1)
-    pool_blocks = latent_cache.reshape(-1, block_size, latent_cache.shape[1])
-    key_rows = jnp.take(pool_blocks, tables, axis=0).reshape(
-        slot_count, block_count * block_size, latent_cache.shape[1]
-    )
-    span = key_rows.shape[1]
-    cached = (
-        jnp.einsum("pshk,stk->psht", queries, key_rows, preferred_element_type=jnp.float32)
-        * score_scale
-    )
-    live = jnp.arange(span, dtype=jnp.int32)[None, :] < slot_len[:, None]
-    cached = jnp.where(live[None, :, None, :], cached, -jnp.inf)
-    current = (
-        jnp.einsum("pshk,nsk->pshn", queries, new_latent, preferred_element_type=jnp.float32)
-        * score_scale
-    )
-    visible = jnp.arange(2, dtype=jnp.int32)[None, :] <= jnp.arange(2, dtype=jnp.int32)[:, None]
-    current = jnp.where(visible[:, None, None, :], current, -jnp.inf)
-    scores = jnp.concatenate([cached, current], axis=3)
-    largest = jnp.max(scores, axis=3, keepdims=True)
-    expo = jnp.exp(scores - largest)
-    weights = (expo / jnp.sum(expo, axis=3, keepdims=True)).astype(jnp.bfloat16)
-    mixed = jnp.einsum(
-        "psht,str->pshr", weights[..., :span], key_rows, preferred_element_type=jnp.float32
-    )[..., :latent_rank]
-    mixed = (
-        mixed
-        + jnp.einsum(
-            "pshn,nsr->pshr", weights[..., span:], new_latent, preferred_element_type=jnp.float32
-        )[..., :latent_rank]
-    )
-    latent_out = mixed.astype(jnp.bfloat16)
-    heads_out = jnp.einsum(
-        "pshr,hrv->pshv", latent_out, value_up, preferred_element_type=jnp.float32
-    ).astype(jnp.bfloat16)
-    heads_out = heads_out.reshape(heads_out.shape[0], slot_count, -1)
 
     def project(portion):
         return jnp.einsum("psv,vd->psd", portion, out_proj, preferred_element_type=jnp.float32)

time: 565 us -> 482 us (0.85)
  local copies, waits for them, and re-layouts: 61.4 us -> 12.2 us
  matrix products: 59.1 us -> 24.8 us
  other arithmetic: 38.5 us -> 6.45 us
  waiting for transfers between devices: 355 us -> 376 us
  Pallas kernels: 0 us -> 12.7 us
    dot_general x5 -> x0, matrix products: 32.4 us -> none  [the longest x1 14 us: shards(): jnp.einsum('pshk,stk->psht', queries, key_rows, preferred_element_type=jn...]
    unnamed x20 -> x27, local copies, waits for them, and re-layouts: 32.4 us -> 7.71 us
    select_n x2 -> x0, other arithmetic: 23.6 us -> none  [shards(): jnp.take(pool_blocks, tables, axis=0)]
    gather x1 -> x0, local copies, waits for them, and re-layouts: 22.1 us -> none  [shards(): jnp.take(pool_blocks, tables, axis=0)]
    all_gather x2, waiting for transfers between devices: 88.1 us -> 108 us  [finish(): partials = project(lax.all_gather(head_block, 'grp', axis=1, tiled=True))]
    pallas_call x0 -> x1, Pallas kernels: none -> 12.7 us  [attend(): pl.pallas_call(attention_kernel, out_shape=jax.ShapeDtypeStruct((2, SLOTS...]
where the time goes in v1:
time: 482 us; the launch traced here: 480 us
  waiting for transfers between devices  376 us (78%)
  blocking collectives  33.5 us (7%)
  matrix products  24.8 us (5%)
  between operations  13.6 us (3%)
  Pallas kernels  12.7 us (3%)
  local copies, waits for them, and re-layouts  12.2 us (3%)
  other arithmetic  6.45 us (1%)
    psum x1, waiting for transfers between devices, finish(): gate_part, up_part = lax.psum((gate_local, up_local), 'grp')  154 us
    all_gather x2, waiting for transfers between devices, finish(): partials = project(lax.all_gather(head_block, 'grp', axis=1, tiled=True))  108 us
    psum x1, waiting for transfers between devices, finish(): attention = lax.psum(partials, 'tp')  59.9 us
    reduce_scatter x2, waiting for transfers between devices, finish(): lax.psum_scatter(jnp.dot(hidden, down_proj, preferred_element_type=jnp.fl...  53.6 us
    psum x1, blocking collectives, finish(): squares = lax.psum(jnp.sum(stream * stream, axis=2), 'grp')  33.5 us
    pallas_call x1, Pallas kernels, attend(): pl.pallas_call(attention_kernel, out_shape=jax.ShapeDtypeStruct((2, SLOTS...  12.7 us
  transfers between devices with their start and end apart: 6, of which 6 were waited for; matrix products, arithmetic and copies ran while one was open for 2% of the time, Pallas kernels for 0%

profile of v1, /device:TPU:1, one launch (start us, length us, event | category | flops | bytes accessed | tf_op | source)
XLA Modules:
  0.0 479.9 jit_solution(3744894713796592999)
XLA Ops:
  6.5 0.9 copy.28
  7.6 1.6 copy-done.1
  9.2 1.3 copy-done.2
  10.5 0.9 copy-done.3
  11.4 0.7 copy-done.4
  12.1 0.7 copy-done.6
  12.7 0.7 copy-done.8
  13.4 12.7 %shard_map.136 = bf16[2,32,2048]{2,1,0:T(8,128)(2,1)S(1)} custom-call(s32[320]{0:T(512)S(1)} %reshape.78.tables, s32[256]{0:T(256)S(1)} %copy-done.4, s32[256]{0:T(256)S(1)} %copy-done.8, s32[16]{0:T(128)S(1)} %copy-done.6, bf16[2,32,16,576]{3,2,1,0:T(8,128)(2,1)S(1)} %copy-done.2, bf16[2,32,576]{2,1,0:T(8,128)(2,1)S(1)} %copy-done.3, ...), custom_call_target="tpu_custom_call" | custom-call | tf_op jit(solution)/shard_map/pallas_call | solution.py:130
  26.1 0.7 fusion.19
  26.9 0.7 all-gather.3.cloned.1.call-update
  28.1 66.9 %all-gather.5.cloned.1.call-done = bf16[1,512,2048]{2,1,0:T(8,128)(2,1)} async-done(((bf16[1,32,2048]{2,1,0:T(8,128)(2,1)}), bf16[1,512,2048]{2,1,0:T(8,128)(2,1)}) %all-gather.5.cloned.1.call-update) | async-done | bytes 2097168 | tf_op jit(solution)/shard_map/all_gather | solution.py:195
  95.0 3.4 fusion
  98.4 1.8 gather_fusion.1
  100.2 41.5 %all-gather.3.cloned.1.call-done = bf16[1,512,2048]{2,1,0:T(8,128)(2,1)} async-done(((bf16[1,32,2048]{2,1,0:T(8,128)(2,1)}), bf16[1,512,2048]{2,1,0:T(8,128)(2,1)}) %all-gather.3.cloned.1.call-update) | async-done | bytes 2097168 | tf_op jit(solution)/shard_map/all_gather | solution.py:195
  141.7 3.4 fusion.2
  145.1 1.8 gather_fusion
  146.9 2.4 bitcast_select_fusion.1
  149.6 0.8 copy.33
  150.4 59.9 %all-reduce.8.cloned.1.call-done = (f32[1,256,448]{2,1,0:T(8,128)}, f32[1,256,448]{2,1,0:T(8,128)}) async-done(((f32[1,256,448]{2,1,0:T(8,128)}, f32[1,256,448]{2,1,0:T(8,128)}), (f32[1,256,448]{2,1,0:T(8,128)}, f32[1,256,448]{2,1,0:T(8,128)})) %all-reduce.8.cloned.1.call-update) | async-done | bytes 917520 | tf_op jit(solution)/shard_map/psum | solution.py:197
  210.3 1.5 multiply_reduce_fusion
  211.8 33.5 %all-reduce = (f32[1,256]{1,0:T(1,128)S(1)}, f32[1,256]{1,0:T(1,128)S(1)}) all-reduce(f32[1,256]{1,0:T(1,128)S(1)} %bitcast.46, f32[1,256]{1,0:T(1,128)S(1)} %bitcast.47), channel_id=1, replica_groups=mesh['grp'=16,'tp'=8] {'grp'}, use_global_device_ids=true, to_apply=%region_11.13 | all-reduce | flops 512 | bytes 4096 | tf_op jit(solution)/shard_map/psum | solution.py:199
  245.3 2.3 fusion.16
  247.5 2.2 fusion.14
  249.8 2.3 fusion.12
  252.1 2.2 fusion.10
  254.4 153.7 %all-reduce.6.cloned.1.call-done = (f32[256,2304]{1,0:T(8,128)}, f32[256,2304]{1,0:T(8,128)}, f32[256,2304]{1,0:T(8,128)}, f32[256,2304]{1,0:T(8,128)}) async-done(((f32[256,2304]{1,0:T(8,128)}, f32[256,2304]{1,0:T(8,128)}, f32[256,2304]{1,0:T(8,128)}, f32[256,2304]{1,0:T(8,128)}), (f32[256,2304]{1,0:T(8,128)}, f32[256,2304]{1,0:T(8,128)}, f32[256,2304]{1,0:T(8,128)}, ...) | async-done | bytes 9437200 | tf_op jit(solution)/shard_map/psum | solution.py:207
  408.1 4.5 convolution_convert_fusion.1
  412.7 4.5 convolution_convert_fusion
  417.2 22.8 %reduce-scatter.3.cloned.1.call-done = bf16[32,448]{1,0:T(8,128)(2,1)} async-done(((bf16[256,448]{1,0:T(8,128)(2,1)}), bf16[32,448]{1,0:T(8,128)(2,1)}) %reduce-scatter.3.cloned.1.call-update) | async-done | bytes 28688 | tf_op jit(solution)/shard_map/reduce_scatter | solution.py:209
  440.1 0.8 fusion.7
  440.8 30.8 %reduce-scatter.5.cloned.1.call-done = bf16[32,448]{1,0:T(8,128)(2,1)} async-done(((bf16[256,448]{1,0:T(8,128)(2,1)}), bf16[32,448]{1,0:T(8,128)(2,1)}) %reduce-scatter.5.cloned.1.call-update) | async-done | bytes 28688 | tf_op jit(solution)/shard_map/reduce_scatter | solution.py:209
  471.6 0.8 fusion.6
  (44 shorter events, 1.7 us)
Async XLA Ops:
  6.5 238.7 %copy-start = (bf16[448,2304]{1,0:T(8,128)(2,1)S(1)}, bf16[448,2304]{1,0:T(8,128)(2,1)}, u32[]{:S(2)}) copy-start(bf16[448,2304]{1,0:T(8,128)(2,1)} %param.27) | copy-start | bytes 6193156
  6.5 88.5 %all-gather.5.cloned.1.call-start = ((), (), s32[]{:S(2)}) async-start(), calls=%async_computation.4 | async-start | bytes 2228224 | tf_op jit(solution)/shard_map/all_gather | solution.py:195
  7.6 1.6 copy-start.1
  9.2 1.3 copy-start.2
  10.5 0.9 copy-start.3
  11.4 0.7 copy-start.4
  12.0 0.7 copy-start.6
  12.7 0.7 copy-start.8
  13.4 14.3 %copy-start.7 = (s32[16]{0:T(128)S(1)}, s32[16]{0:T(128)}, u32[]{:S(2)}) copy-start(s32[16]{0:T(128)} %rows.1) | copy-start | bytes 196
  13.4 14.5 %copy-start.5 = (s32[256]{0:T(256)S(1)}, s32[256]{0:T(256)}, u32[]{:S(2)}) copy-start(s32[256]{0:T(256)} %order.1) | copy-start | bytes 3076
  26.9 114.9 %all-gather.3.cloned.1.call-start = ((), (), s32[]{:S(2)}) async-start(), calls=%async_computation.2 | async-start | bytes 2228224 | tf_op jit(solution)/shard_map/all_gather | solution.py:195
  27.6 182.7 %all-reduce.8.cloned.1.call-start = ((), (), s32[]{:S(2)}) async-start(), calls=%async_computation.7 | async-start | bytes 2097152 | tf_op jit(solution)/shard_map/psum | solution.py:197
  146.9 2.5 copy-start.10
  146.9 3.5 copy-start.11
  149.4 258.7 %all-reduce.6.cloned.1.call-start = ((), (), s32[]{:S(2)}) async-start(), calls=%async_computation.6 | async-start | bytes 18874368 | tf_op jit(solution)/shard_map/psum | solution.py:207
  245.3 2.3 copy-start.9
  254.3 185.7 %reduce-scatter.3.cloned.1.call-start = ((), (), s32[]{:S(2)}) async-start(), calls=%async_computation.3 | async-start | bytes 294912 | tf_op jit(solution)/shard_map/reduce_scatter | solution.py:209
  412.6 59.0 %reduce-scatter.5.cloned.1.call-start = ((), (), s32[]{:S(2)}) async-start(), calls=%async_computation.5 | async-start | bytes 294912 | tf_op jit(solution)/shard_map/reduce_scatter | solution.py:209
Sparse Core Ops, SparseCore 0:
  27.0 68.0 all-gather.4
  97.2 44.5 all-gather.2
  149.5 60.7 all-reduce.7
  254.5 153.5 all-reduce.5
  412.7 27.2 reduce-scatter.2
  442.3 29.3 reduce-scatter.4

commit v2 on v1

--- a/solution.py
+++ b/solution.py
@@ -1,5 +1,3 @@
-import functools
-
 import jax
 import jax.numpy as jnp
 from jax import lax
@@ -153,13 +151,427 @@
     )
 
 
-def slot_positions(group_rows, request_order, slot_count):
-    group_ends = jnp.cumsum(group_rows)
-    group_starts = group_ends - group_rows
-    group_of = jnp.sum((request_order[:, None] >= group_ends[None, :]).astype(jnp.int32), axis=1)
-    in_group = group_of[:, None] == jnp.arange(group_rows.shape[0], dtype=jnp.int32)[None, :]
-    first_slot = jnp.sum(jnp.where(in_group, group_starts[None, :], 0), axis=1)
-    return group_of * slot_count + request_order - first_slot
+MESH = pl.DeviceIdType.MESH
+WIDE = 512
+COLS = 448
+FFT = 2304
+TAIL = 128
+BF16 = jnp.bfloat16
+F32 = jnp.float32
+
+
+def layer_kernel(
+    heads,
+    order_ref,
+    rows_ref,
+    residual,
+    gain_ref,
+    wo_hbm,
+    wg_hbm,
+    wu_hbm,
+    wd_hbm,
+    out_ref,
+    wo,
+    wg,
+    wu,
+    wd,
+    res,
+    gathered,
+    hiddens,
+    select,
+    stream,
+    part,
+    from_core,
+    summed,
+    from_x,
+    normed,
+    chunks_a,
+    chunks_b,
+    relay_a,
+    relay_b,
+    final_a,
+    final_b,
+    line_a,
+    line_b,
+    relay2_a,
+    relay2_b,
+    final2_a,
+    final2_b,
+    local_sems,
+    send_sems,
+    recv_sems,
+):
+    g, t = lax.axis_index("grp"), lax.axis_index("tp")
+    y, z = g // 4, lax.rem(g, 4)
+    x, core = t // 2, lax.rem(t, 2)
+
+    def group_at(dy, dz):
+        return lax.rem(y + dy + 4, 4) * 4 + lax.rem(z + dz + 4, 4)
+
+    def tp_at(dx):
+        return lax.rem(x + dx + 4, 4) * 2 + core
+
+    partner = x * 2 + 1 - core
+    used = []
+
+    def remote(src, dst, device):
+        i = len(used)
+        copy = pltpu.make_async_remote_copy(
+            src_ref=src,
+            dst_ref=dst,
+            send_sem=send_sems.at[i],
+            recv_sem=recv_sems.at[i],
+            device_id=device,
+            device_id_type=MESH,
+        )
+        copy.start()
+        used.append(copy)
+        return copy
+
+    local = []
+
+    def bring(src, dst):
+        copy = pltpu.make_async_copy(src, dst, local_sems.at[len(local)])
+        copy.start()
+        local.append(copy)
+        return copy
+
+    heads_in = [bring(heads.at[:, :, pl.ds(h * 1024, 1024)], gathered.at[h, g]) for h in range(2)]
+    wo_in = bring(wo_hbm, wo)
+    res_in = bring(residual, res)
+    wg_in = bring(wg_hbm, wg)
+    wu_in = bring(wu_hbm, wu)
+    wd_in = bring(wd_hbm, wd)
+
+    barrier = pltpu.get_barrier_semaphore()
+    greet = [(group_at(dy, dz), t) for dy, dz in ((1, 0), (-1, 0), (0, 1), (0, -1))]
+    greet += [(g, tp_at(1)), (g, tp_at(-1)), (g, tp_at(2)), (g, partner)]
+    for device in greet:
+        pl.semaphore_signal(barrier, inc=1, device_id=device, device_id_type=MESH)
+    pl.semaphore_wait(barrier, len(greet))
+
+    def all_gather(bufs):
+        def slot(h, da, db):
+            return group_at(da, db) if h == 0 else group_at(db, da)
+
+        def send(h, da, db, to_a, to_b, half=None):
+            at = slot(h, da, db)
+            ref = bufs[h].at[at] if half is None else bufs[h].at[at, half]
+            return remote(ref, ref, (slot(h, to_a, to_b), t))
+
+        along = [{}, {}]
+        up, down, up2, down2 = [{}, {}], [{}, {}], [{}, {}], [{}, {}]
+
+        def across(h, d):
+            up[h][d] = send(h, d, 0, 0, 1)
+            down[h][d] = send(h, d, 0, 0, -1)
+
+        def pass_on(h, d):
+            up[h][d].wait_recv()
+            up2[h][d] = send(h, d, -1, 0, 1, 0)
+            down[h][d].wait_recv()
+            down2[h][d] = send(h, d, 1, 0, -1, 1)
+
+        for h in range(2):
+            along[h]["+"] = send(h, 0, 0, 1, 0)
+            along[h]["-"] = send(h, 0, 0, -1, 0)
+            across(h, 0)
+        for h in range(2):
+            along[h]["+"].wait_recv()
+            along[h]["++"] = send(h, -1, 0, 1, 0, 0)
+            across(h, -1)
+            along[h]["-"].wait_recv()
+            along[h]["--"] = send(h, 1, 0, -1, 0, 1)
+            across(h, 1)
+        for h in range(2):
+            pass_on(h, 0)
+        for h in range(2):
+            along[h]["++"].wait_recv()
+            along[h]["--"].wait_recv()
+            across(h, 2)
+        for d in (-1, 1, 2):
+            for h in range(2):
+                pass_on(h, d)
+        for d in (0, -1, 1, 2):
+            for h in range(2):
+                up2[h][d].wait_recv()
+                down2[h][d].wait_recv()
+
+    def scatter_tp(turn):
+        to_core = remote(part.at[turn, 1 - core], from_core.at[turn], (g, partner))
+        to_core.wait_recv()
+        for k in range(4):
+            summed[turn, k] = (
+                part[turn, core, k].astype(F32) + from_core[turn, k].astype(F32)
+            ).astype(BF16)
+        moves = []
+        for i, dx in enumerate((1, -1, 2)):
+            chip = lax.rem(x + dx + 4, 4)
+            moves.append(remote(summed.at[turn, chip], from_x.at[turn, i], (g, tp_at(dx))))
+        total = summed[turn, x].astype(F32)
+        for i, move in enumerate(moves):
+            move.wait_recv()
+            total = total + from_x[turn, i].astype(F32)
+        return total[:, :COLS]
+
+    for copy in heads_in:
+        copy.wait()
+    all_gather([gathered.at[0], gathered.at[1]])
+
+    spread = lax.broadcasted_iota(jnp.int32, (GRPS, GRPS), 1)
+    row_of = lax.broadcasted_iota(jnp.int32, (GRPS, GRPS), 0)
+    ends = jnp.sum(jnp.where(spread <= row_of, rows_ref[...], 0), axis=1, keepdims=True)
+    starts = jnp.sum(jnp.where(spread < row_of, rows_ref[...], 0), axis=1, keepdims=True)
+    order = order_ref[...]
+    in_group = jnp.logical_and(order >= starts, order < ends)
+    group_id = lax.broadcasted_iota(jnp.int32, (GRPS, REQS), 0)
+    at = jnp.sum(jnp.where(in_group, group_id * SLOTS + order - starts, 0), axis=0, keepdims=True)
+    matches = lax.broadcasted_iota(jnp.int32, (GRPS * SLOTS, REQS), 0) == at
+    select[...] = jnp.where(matches, 1.0, 0.0).astype(BF16)
+
+    wo_in.wait()
+    part[:, :, :, :, 384:] = jnp.zeros(part.shape[:-1] + (128,), BF16)
+    TN = (((0,), (0,)), ((), ()))
+    for s in range(2):
+        rows = []
+        for q in range(2):
+            both = [gathered[h, pl.ds(8 * q, 8), s].reshape(8 * SLOTS, 1024) for h in range(2)]
+            value = lax.dot_general(both[0], wo[:, :1024], NT, preferred_element_type=F32)
+            value = value + lax.dot_general(both[1], wo[:, 1024:], NT, preferred_element_type=F32)
+            rows.append(value.astype(BF16))
+        value = jnp.concatenate(rows, axis=0)
+        placed = lax.dot_general(select[...], value, TN, preferred_element_type=F32).astype(BF16)
+        for k in range(8):
+            part[0, k % 2, k // 2, s * 32 : s * 32 + 32, :COLS] = placed[32 * k : 32 * k + 32]
+    attention = scatter_tp(0)
+
+    res_in.wait()
+    mine = lax.broadcasted_iota(jnp.int32, (32, REQS), 1) == (
+        lax.broadcasted_iota(jnp.int32, (32, REQS), 0) + t * 32
+    )
+    mine = jnp.where(mine, 1.0, 0.0).astype(BF16)
+    for s in range(2):
+        own = lax.dot_general(mine, res[s], NT, preferred_element_type=F32)
+        stream[s * 32 : s * 32 + 32, :] = own + attention[s * 32 : s * 32 + 32]
+    here = stream[...]
+    squares = jnp.sum(here * here, axis=1, keepdims=True)
+    high = squares.astype(BF16)
+    low = (squares - high.astype(F32)).astype(BF16)
+    lane = lax.broadcasted_iota(jnp.int32, (64, WIDE - COLS), 1)
+    extra = jnp.where(lane == 0, high, jnp.where(lane == 1, low, jnp.zeros_like(high)))
+    scaled = (here * gain_ref[...].astype(F32)).astype(BF16)
+    scaled = jnp.concatenate([scaled, extra], axis=1)
+    normed[2 * t] = scaled[:32]
+    normed[2 * t + 1] = scaled[32:]
+
+    def pair(index):
+        return normed.at[pl.ds(2 * index, 2)]
+
+    moves = [remote(pair(t), pair(t), (g, tp_at(dx))) for dx in (1, -1, 2)]
+    moves.append(remote(pair(t), pair(t), (g, partner)))
+    shares = []
+    for move, dx in zip(moves[:3], (-1, 1, 2)):
+        move.wait_recv()
+        shares.append(remote(pair(tp_at(dx)), pair(tp_at(dx)), (g, partner)))
+    for move in moves[3:] + shares:
+        move.wait_recv()
+    wg_in.wait()
+    wu_in.wait()
+
+    chunks, weight = (chunks_a, chunks_b), (wg, wu)
+    relay, final, line = (relay_a, relay_b), (final_a, final_b), (line_a, line_b)
+    relay2, final2 = (relay2_a, relay2_b), (final2_a, final2_b)
+    cut = (1280, 1152)
+    first = (pl.ds(0, 1280), pl.ds(0, 1152))
+    second = (pl.ds(1280, 1152), pl.ds(1152, 1152))
+
+    def along(h, d):
+        return (group_at(d, 0) if h == 0 else group_at(0, d), t)
+
+    def across(h, d):
+        return along(1 - h, d)
+
+    def product(h, i, d):
+        blocks = []
+        for k in range(4):
+            b = lax.rem(y + d + 4, 4) * 4 + k if h == 0 else k * 4 + lax.rem(z + d + 4, 4)
+            blocks.append(normed[b])
+        rows = jnp.concatenate(blocks, axis=0)
+        if h == 0:
+            chunks[h][i, :, FFT:] = rows[:, 384:]
+        rows = rows[:, :COLS]
+
+        def one(n, carry):
+            at = pl.ds(pl.multiple_of(n * 256, 256), 256)
+            chunks[h][i, :, at] = jnp.dot(
+                rows, weight[h][:, at], preferred_element_type=F32
+            ).astype(BF16)
+            return carry
+
+        lax.fori_loop(0, FFT // 256, one, 0)
+
+    def add(ref, index, part_cols, other):
+        ref[index, :, part_cols] = (
+            ref[index, :, part_cols].astype(F32) + other[...].astype(F32)
+        ).astype(BF16)
+
+    relays, finals = [None, None], [[], []]
+    for h in range(2):
+        product(h, 2, 2)
+        relays[h] = (
+            remote(chunks[h].at[2, :, first[h]], relay[h].at[0, :, first[h]], along(h, 1)),
+            remote(chunks[h].at[2, :, second[h]], relay[h].at[1, :, pl.ds(0, 1152)], along(h, -1)),
+        )
+    for h in range(2):
+        product(h, 1, 1)
+        finals[h].append(
+            remote(chunks[h].at[1, :, second[h]], final[h].at[0, :, second[h]], along(h, 1))
+        )
+        product(h, 3, -1)
+        finals[h].append(
+            remote(chunks[h].at[3, :, first[h]], final[h].at[1, :, first[h]], along(h, -1))
+        )
+    for h in range(2):
+        relays[h][0].wait_recv()
+        add(chunks[h], 1, first[h], relay[h].at[0, :, first[h]])
+        finals[h].append(
+            remote(chunks[h].at[1, :, first[h]], final[h].at[0, :, first[h]], along(h, 1))
+        )
+        relays[h][1].wait_recv()
+        add(chunks[h], 3, second[h], relay[h].at[1, :, pl.ds(0, 1152)])
+        finals[h].append(
+            remote(chunks[h].at[3, :, second[h]], final[h].at[1, :, second[h]], along(h, -1))
+        )
+    for h in range(2):
+        product(h, 0, 0)
+    relays, finals2 = [None, None], [[], []]
+    for h in range(2):
+        for copy in finals[h]:
+            copy.wait_recv()
+        for k in range(4):
+            at = pl.ds(32 * k, 32)
+            line[h][k] = (
+                chunks[h][0, at, :].astype(F32)
+                + final[h][0, at, :].astype(F32)
+                + final[h][1, at, :].astype(F32)
+            ).astype(BF16)
+        spot = z if h == 0 else y
+
+        def place(d):
+            return lax.rem(spot + d + 4, 4)
+
+        far, ahead, behind = place(2), place(1), place(-1)
+        relays[h] = (
+            remote(line[h].at[far, :, first[h]], relay2[h].at[0, :, first[h]], across(h, 1)),
+            remote(line[h].at[far, :, second[h]], relay2[h].at[1, :, pl.ds(0, 1152)], across(h, -1)),
+        )
+        finals2[h].append(
+            remote(line[h].at[ahead, :, second[h]], final2[h].at[0, :, second[h]], across(h, 1))
+        )
+        finals2[h].append(
+            remote(line[h].at[behind, :, first[h]], final2[h].at[1, :, first[h]], across(h, -1))
+        )
+    totals = []
+    for h in range(2):
+        spot = z if h == 0 else y
+        ahead, behind = lax.rem(spot + 1, 4), lax.rem(spot + 3, 4)
+        relays[h][0].wait_recv()
+        add(line[h], ahead, first[h], relay2[h].at[0, :, first[h]])
+        finals2[h].append(
+            remote(line[h].at[ahead, :, first[h]], final2[h].at[0, :, first[h]], across(h, 1))
+        )
+        relays[h][1].wait_recv()
+        add(line[h], behind, second[h], relay2[h].at[1, :, pl.ds(0, 1152)])
+        finals2[h].append(
+            remote(line[h].at[behind, :, second[h]], final2[h].at[1, :, second[h]], across(h, -1))
+        )
+    for h in range(2):
+        for copy in finals2[h]:
+            copy.wait_recv()
+        spot = z if h == 0 else y
+        totals.append(
+            line[h][spot].astype(F32) + final2[h][0].astype(F32) + final2[h][1].astype(F32)
+        )
+    mean = (totals[0][:, FFT + 64 : FFT + 65] + totals[0][:, FFT + 65 : FFT + 66]) / D
+    inverse_rms = lax.rsqrt(mean + 1e-06)
+    gate = totals[0][:, :FFT] * inverse_rms
+    up = totals[1] * inverse_rms
+    hidden = (gate / (1.0 + jnp.exp(-gate)) * up).astype(BF16)
+    for h in range(2):
+        for k in range(2):
+            hiddens[h, g, k] = hidden[16 * k : 16 * k + 16, 1152 * h : 1152 * h + 1152]
+    all_gather([hiddens.at[0], hiddens.at[1]])
+
+    wd_in.wait()
+    for q in range(4):
+        both = [hiddens[h, 4 * q : 4 * q + 4].reshape(128, 1152) for h in range(2)]
+        value = lax.dot_general(both[0], wd[:, :1152], NT, preferred_element_type=F32)
+        value = value + lax.dot_general(both[1], wd[:, 1152:], NT, preferred_element_type=F32)
+        value = value.astype(BF16)
+        for k in range(2):
+            part[1, k, q, :, :COLS] = value[64 * k : 64 * k + 64]
+    reduced = scatter_tp(1)
+    for s in range(2):
+        at = slice(32 * s, 32 * s + 32)
+        out_ref[s] = (stream[at, :] + reduced[at]).astype(BF16)
+    for copy in used:
+        copy.wait_send()
+
+
+def layer(heads, request_order, group_rows, residual, norm_gain, out_proj, gate_proj, up_proj, down_proj):
+    vmem = pl.BlockSpec(memory_space=pltpu.VMEM)
+    hbm = pl.BlockSpec(memory_space=pl.ANY)
+    copies = 40 + 40 + 4 + 4 + 4 + 3 + 12 + 12
+    return pl.pallas_call(
+        layer_kernel,
+        out_shape=jax.ShapeDtypeStruct((2, 32, COLS), BF16),
+        in_specs=[hbm, vmem, vmem, hbm, vmem, hbm, hbm, hbm, hbm],
+        out_specs=vmem,
+        scratch_shapes=[
+            pltpu.VMEM((COLS, 2048), BF16),
+            pltpu.VMEM((COLS, FFT), BF16),
+            pltpu.VMEM((COLS, FFT), BF16),
+            pltpu.VMEM((COLS, FFT), BF16),
+            pltpu.VMEM((2, COLS, REQS), BF16),
+            pltpu.VMEM((2, GRPS, 2, SLOTS, 1024), BF16),
+            pltpu.VMEM((2, GRPS, 2, 16, 1152), BF16),
+            pltpu.VMEM((GRPS * SLOTS, REQS), BF16),
+            pltpu.VMEM((64, COLS), F32),
+            pltpu.VMEM((2, 2, 4, 64, WIDE), BF16),
+            pltpu.VMEM((2, 4, 64, WIDE), BF16),
+            pltpu.VMEM((2, 4, 64, WIDE), BF16),
+            pltpu.VMEM((2, 3, 64, WIDE), BF16),
+            pltpu.VMEM((16, 32, WIDE), BF16),
+            pltpu.VMEM((4, 128, FFT + TAIL), BF16),
+            pltpu.VMEM((4, 128, FFT), BF16),
+            pltpu.VMEM((2, 128, 1280), BF16),
+            pltpu.VMEM((2, 128, 1152), BF16),
+            pltpu.VMEM((2, 128, FFT + TAIL), BF16),
+            pltpu.VMEM((2, 128, FFT), BF16),
+            pltpu.VMEM((4, 32, FFT + TAIL), BF16),
+            pltpu.VMEM((4, 32, FFT), BF16),
+            pltpu.VMEM((2, 32, 1280), BF16),
+            pltpu.VMEM((2, 32, 1152), BF16),
+            pltpu.VMEM((2, 32, FFT + TAIL), BF16),
+            pltpu.VMEM((2, 32, FFT), BF16),
+            pltpu.SemaphoreType.DMA((7,)),
+            pltpu.SemaphoreType.DMA((copies,)),
+            pltpu.SemaphoreType.DMA((copies,)),
+        ],
+        compiler_params=pltpu.CompilerParams(
+            collective_id=0, has_side_effects=True, vmem_limit_bytes=56 << 20
+        ),
+    )(
+        heads,
+        request_order.reshape(1, REQS),
+        group_rows.reshape(1, GRPS),
+        jnp.swapaxes(residual, 1, 2),
+        norm_gain.reshape(1, COLS),
+        out_proj.T,
+        gate_proj,
+        up_proj,
+        down_proj.T,
+    )
 
 
 def shards(
@@ -178,52 +590,20 @@
     up_proj,
     down_proj,
 ):
-    slot_count = tables.shape[0]
-    requests = request_order.shape[0]
-    tp_count = lax.axis_size("tp")
-    my_requests = requests // tp_count
-    heads_out = attend(
+    heads = attend(
         queries, new_latent, latent_cache, tables, context_len, group_rows, request_order, value_up
     )
-    slot_index = slot_positions(group_rows, request_order, slot_count)
-
-    def project(portion):
-        return jnp.einsum("psv,vd->psd", portion, out_proj, preferred_element_type=jnp.float32)
-
-    def finish(head_block, residual_block):
-        step_count = head_block.shape[0]
-        partials = project(lax.all_gather(head_block, "grp", axis=1, tiled=True))
-        partials = jnp.take(partials, slot_index, axis=1)
-        attention = lax.psum(partials, "tp")
-        stream = residual_block.astype(jnp.float32) + attention
-        squares = lax.psum(jnp.sum(stream * stream, axis=2), "grp")
-        inverse_rms = lax.rsqrt(squares / D + 1e-06)
-        normed = (stream * inverse_rms[..., None] * norm_gain.astype(jnp.float32)).astype(
-            jnp.bfloat16
-        )
-        normed = jnp.swapaxes(normed, 0, 1).reshape(requests * step_count, -1)
-        gate_local = jnp.dot(normed, gate_proj, preferred_element_type=jnp.float32)
-        up_local = jnp.dot(normed, up_proj, preferred_element_type=jnp.float32)
-        gate_part, up_part = lax.psum((gate_local, up_local), "grp")
-        hidden = (jax.nn.silu(gate_part) * up_part).astype(jnp.bfloat16)
-        reduced = lax.psum_scatter(
-            jnp.dot(hidden, down_proj, preferred_element_type=jnp.float32).astype(jnp.bfloat16),
-            "tp",
-            scatter_dimension=0,
-            tiled=True,
-        ).astype(jnp.float32)
-        reduced = jnp.swapaxes(reduced.reshape(my_requests, step_count, -1), 0, 1)
-        mine = lax.dynamic_slice_in_dim(stream, lax.axis_index("tp") * my_requests, my_requests, 1)
-        return (mine + reduced).astype(jnp.bfloat16)
-
-    layer_out = jnp.concatenate(
-        [
-            finish(heads_out[step_index : step_index + 1], residual[step_index : step_index + 1])
-            for step_index in range(2)
-        ],
-        axis=0,
+    return layer(
+        heads,
+        request_order,
+        group_rows,
+        residual,
+        norm_gain,
+        out_proj,
+        gate_proj,
+        up_proj,
+        down_proj,
     )
-    return layer_out
 
 
 def solution(mesh):

time: 482 us -> 157 us (0.33)
  waiting for transfers between devices: 376 us -> 0 us
  Pallas kernels: 12.7 us -> 147 us
  blocking collectives: 33.5 us -> 0 us
  matrix products: 24.8 us -> 0 us
  between operations: 13.6 us -> 0.04 us
  other arithmetic: 6.45 us -> 0 us
    psum x2 -> x0, waiting for transfers between devices: 214 us -> none  [the longest x1 154 us: finish(): gate_part, up_part = lax.psum((gate_local, up_local), 'grp')]
    pallas_call x0 -> x1, Pallas kernels: none -> 120 us  [layer(): pl.pallas_call(layer_kernel, out_shape=jax.ShapeDtypeStruct((2, 32, COLS)...]
    all_gather x2 -> x0, waiting for transfers between devices: 108 us -> none  [finish(): partials = project(lax.all_gather(head_block, 'grp', axis=1, tiled=True))]
    reduce_scatter x2 -> x0, waiting for transfers between devices: 53.6 us -> none  [finish(): lax.psum_scatter(jnp.dot(hidden, down_proj, preferred_element_type=jnp.fl...]
    psum x1 -> x0, blocking collectives: 33.5 us -> none  [finish(): squares = lax.psum(jnp.sum(stream * stream, axis=2), 'grp')]
    dot_general x6 -> x0, matrix products: 18.1 us -> none  [the longest x2 9.04 us: finish(): jnp.dot(hidden, down_proj, preferred_element_type=jnp.float32)]
    pallas_call x1, Pallas kernels: 12.7 us -> 26.9 us  [attend(): pl.pallas_call(attention_kernel, out_shape=jax.ShapeDtypeStruct((2, SLOTS...]
    another operation x2 -> x0, matrix products: 6.79 us -> none  [finish(): partials = jnp.take(partials, slot_index, axis=1)]
  transfers between devices with their start and end apart: 6 -> 0, of which waited for: 6 -> 0; matrix products, arithmetic and copies ran while one was open for 2% -> 0% of each run, Pallas kernels for 0% -> 0%
where the time goes in v2:
time: 157 us
  Pallas kernels  147 us (94%)
  local copies, waits for them, and re-layouts  10.1 us (6%)
    pallas_call x1, Pallas kernels, layer(): pl.pallas_call(layer_kernel, out_shape=jax.ShapeDtypeStruct((2, 32, COLS)...  120 us
    pallas_call x1, Pallas kernels, attend(): pl.pallas_call(attention_kernel, out_shape=jax.ShapeDtypeStruct((2, SLOTS...  26.9 us
    unnamed x16, local copies, waits for them, and re-layouts  8.74 us

profile of v2, /device:TPU:1, one launch (start us, length us, event | category | flops | bytes accessed | tf_op | source)
XLA Modules:
  0.0 157.0 jit_solution(1119095914141101191)
XLA Ops:
  0.0 1.3 reshape.15.gain_ref
  1.3 0.8 copy.15
  2.0 0.1 reshape.12.tables
  2.1 0.0 copy-start
  2.2 1.6 %copy-done = bf16[16,512,128]{2,1,0:T(8,128)(2,1)S(1)} copy-done((bf16[16,512,128]{2,1,0:T(8,128)(2,1)S(1)}, bf16[16,512,128]{2,1,0:T(8,128)(2,1)}, u32[]{:S(2)}) %copy-start) | copy-done | bytes 2097176
  3.7 0.0 copy-start.1
  3.7 1.3 copy-done.1
  5.1 0.0 copy-start.3
  5.1 0.9 copy-done.3
  5.9 0.0 copy-start.4
  5.9 0.7 copy-done.4
  6.6 0.0 copy-start.5
  6.6 0.7 copy-done.5
  7.3 0.0 copy-start.6
  7.3 0.7 copy-done.6
  8.0 26.9 %shard_map.136.heads = bf16[2,32,2048]{2,1,0:T(8,128)(2,1)S(1)} custom-call(s32[320]{0:T(512)S(1)} %reshape.12.tables, s32[256]{0:T(256)S(1)} %copy-done.4, s32[256]{0:T(256)S(1)} %copy-done.6, s32[16]{0:T(128)S(1)} %copy-done.5, bf16[2,32,16,576]{3,2,1,0:T(8,128)(2,1)S(1)} %copy-done.1, bf16[2,32,576]{2,1,0:T(8,128)(2,1)S(1)} %copy-done.3, ...), custom_call_target="tpu_custom_call" | custom-call | tf_op jit(solution)/shard_map/pallas_call | solution.py:128
  34.8 0.0 copy-start.2
  34.8 0.7 copy-done.2
  35.5 120.0 %shard_map.137 = bf16[2,32,448]{2,1,0:T(8,128)(2,1)} custom-call(bf16[2,32,2048]{2,1,0:T(8,128)(2,1)} %copy-done.2, s32[1,256]{1,0:T(1,128)} %bitcast.6, s32[1,16]{1,0:T(1,128)} %bitcast.7, bf16[2,448,256]{2,1,0:T(8,128)(2,1)} %bitcast.11, bf16[1,448]{1,0:T(2,128)(2,1)} %reshape.15.gain_ref, bf16[448,2048]{1,0:T(8,128)(2,1)} %bitcast.10, ...), custom_call_target="tpu_custom_call" | custom-call | tf_op jit(solution)/shard_map/pallas_call | solution.py:525
  155.6 1.5 copy.17
Async XLA Ops:
  2.1 1.6 %copy-start = (bf16[16,512,128]{2,1,0:T(8,128)(2,1)S(1)}, bf16[16,512,128]{2,1,0:T(8,128)(2,1)}, u32[]{:S(2)}) copy-start(bf16[16,512,128]{2,1,0:T(8,128)(2,1)} %vup_ref.1) | copy-start | bytes 6291460
  3.7 1.3 copy-start.1
  5.1 0.9 copy-start.3
  5.9 0.7 copy-start.4
  6.6 0.7 copy-start.5
  7.3 0.7 copy-start.6
  34.8 0.7 copy-start.2

commit v3 on v2

--- a/solution.py
+++ b/solution.py
@@ -9,147 +9,22 @@
 SLOTS = 32
 BLOCKS = 10
 BLOCK = 64
-SPAN = BLOCKS * BLOCK
 HEADS = 16
 KDIM = 576
 RANK = 512
 VH = 128
 GRPS = 16
 REQS = 256
+POOL = 320
+BATCH = 8
+BATCHES = SLOTS // BATCH
+PIECE = 10
+PIECES = POOL // 2 // PIECE
+RING = 3
 
 score_scale = 192.0 ** (-0.5)
 NT = (((1,), (1,)), ((), ()))
-
-
-def attention_kernel(
-    tables, order, ctx, rows, q_ref, new_ref, cache, vup_ref, out_ref, raw, keys, lat, fresh_all, lens, sems
-):
-    group = lax.axis_index("grp")
-
-    def add_rows(j, total):
-        return total + jnp.where(j < group, rows[j], 0)
-
-    start = lax.fori_loop(0, GRPS, add_rows, 0)
-    live = rows[group]
-
-    def clear(i, carry):
-        lens[i] = 0
-        return carry
-
-    lax.fori_loop(0, SLOTS + 1, clear, 0)
-
-    def put_len(r, carry):
-        where = order[r] - start
-        inside = jnp.logical_and(where >= 0, where < live)
-        lens[jnp.where(inside, where, SLOTS)] = ctx[r]
-        return carry
-
-    lax.fori_loop(0, REQS, put_len, 0, unroll=8)
-
-    def copies(pair, buf, action):
-        for k in range(2):
-            slot = pair * 2 + k
-            count = jnp.where(slot < live, (lens[slot] + BLOCK - 1) // BLOCK, 0)
-            for j in range(BLOCKS):
-
-                @pl.when(j < count)
-                def _():
-                    block = tables[slot * BLOCKS + j]
-                    first = pl.multiple_of((block // 2) * (2 * BLOCK), 2 * BLOCK)
-                    action(
-                        pltpu.make_async_copy(
-                            cache.at[:, pl.ds(first, 2 * BLOCK)],
-                            raw.at[buf, k * BLOCKS + j],
-                            sems.at[buf, k * BLOCKS + j],
-                        )
-                    )
-
-    pairs = (live + 1) // 2
-    raw[...] = jnp.zeros_like(raw)
-    copies(0, 0, lambda c: c.start())
-    lat[...] = jnp.zeros_like(lat)
-    fresh_all[...] = new_ref[...].astype(jnp.float32)
-    low = lax.broadcasted_iota(jnp.int32, (KDIM, 2 * BLOCK), 1) < BLOCK
-    position = lax.broadcasted_iota(jnp.int32, (2 * HEADS, SPAN), 1)
-    step_of = lax.broadcasted_iota(jnp.int32, (2 * HEADS, 1), 0) // HEADS
-
-    def one_pair(pair, carry):
-        buf = lax.rem(pair, 2)
-        copies(pair, buf, lambda c: c.wait())
-
-        @pl.when(pair + 1 < pairs)
-        def _():
-            copies(pair + 1, 1 - buf, lambda c: c.start())
-
-        for k in range(2):
-            slot = pair * 2 + k
-            for j in range(BLOCKS // 2):
-                odd_a = lax.rem(tables[slot * BLOCKS + 2 * j], 2)
-                odd_b = lax.rem(tables[slot * BLOCKS + 2 * j + 1], 2)
-                a = raw[buf, k * BLOCKS + 2 * j]
-                b = raw[buf, k * BLOCKS + 2 * j + 1]
-                a = pltpu.roll(a, odd_a * BLOCK, 1)
-                b = pltpu.roll(b, (1 - odd_b) * BLOCK, 1)
-                keys[k, :, j * 128 : (j + 1) * 128] = jnp.where(low, a, b)
-        for k in range(2):
-            slot = pair * 2 + k
-            q = q_ref[:, slot].reshape(2 * HEADS, KDIM)
-            fresh_float = [fresh_all[t, pl.ds(slot, 1), :] for t in range(2)]
-            scores = jnp.dot(q, keys[k], preferred_element_type=jnp.float32) * score_scale
-            scores = jnp.where(position < lens[slot], scores, -jnp.inf)
-            q_float = q.astype(jnp.float32)
-            now = jnp.sum(q_float * fresh_float[0], axis=1, keepdims=True) * score_scale
-            later = jnp.sum(q_float * fresh_float[1], axis=1, keepdims=True) * score_scale
-            later = jnp.where(step_of == 1, later, -jnp.inf)
-            largest = jnp.maximum(jnp.max(scores, axis=1, keepdims=True), jnp.maximum(now, later))
-            expo = jnp.exp(scores - largest)
-            now = jnp.exp(now - largest)
-            later = jnp.exp(later - largest)
-            inverse = 1.0 / (jnp.sum(expo, axis=1, keepdims=True) + now + later)
-            mixed = lax.dot_general(
-                expo.astype(jnp.bfloat16), keys[k, :RANK, :], NT, preferred_element_type=jnp.float32
-            )
-            mixed = mixed + now * fresh_float[0][:, :RANK] + later * fresh_float[1][:, :RANK]
-            lat[slot] = mixed * inverse
-        return carry
-
-    lax.fori_loop(0, pairs, one_pair, 0)
-
-    for h in range(HEADS):
-        both = jnp.concatenate([lat[:, h, :], lat[:, HEADS + h, :]], axis=0).astype(jnp.bfloat16)
-        value = jnp.dot(both, vup_ref[h], preferred_element_type=jnp.float32).astype(jnp.bfloat16)
-        out_ref[0, :, h * VH : (h + 1) * VH] = value[:SLOTS]
-        out_ref[1, :, h * VH : (h + 1) * VH] = value[SLOTS:]
-
-
-def attend(queries, new_latent, latent_cache, tables, context_len, group_rows, request_order, value_up):
-    smem = pl.BlockSpec(memory_space=pltpu.SMEM)
-    vmem = pl.BlockSpec(memory_space=pltpu.VMEM)
-    return pl.pallas_call(
-        attention_kernel,
-        out_shape=jax.ShapeDtypeStruct((2, SLOTS, HEADS * VH), jnp.bfloat16),
-        in_specs=[smem] * 4 + [vmem, vmem, pl.BlockSpec(memory_space=pl.ANY), vmem],
-        out_specs=vmem,
-        scratch_shapes=[
-            pltpu.VMEM((2, 2 * BLOCKS, KDIM, 2 * BLOCK), jnp.bfloat16),
-            pltpu.VMEM((2, KDIM, SPAN), jnp.bfloat16),
-            pltpu.VMEM((SLOTS, 2 * HEADS, RANK), jnp.float32),
-            pltpu.VMEM((2, SLOTS, KDIM), jnp.float32),
-            pltpu.SMEM((SLOTS + 1,), jnp.int32),
-            pltpu.SemaphoreType.DMA((2, 2 * BLOCKS)),
-        ],
-        compiler_params=pltpu.CompilerParams(vmem_limit_bytes=40 << 20),
-    )(
-        tables.reshape(-1),
-        request_order,
-        context_len,
-        group_rows,
-        queries,
-        new_latent,
-        latent_cache.T,
-        value_up,
-    )
-
+TN = (((0,), (0,)), ((), ()))
 
 MESH = pl.DeviceIdType.MESH
 WIDE = 512
@@ -161,16 +36,38 @@
 
 
 def layer_kernel(
-    heads,
-    order_ref,
-    rows_ref,
+    queries,
+    fresh_hbm,
+    cache,
+    tables_hbm,
+    lengths_hbm,
+    rows_hbm,
+    order_hbm,
     residual,
-    gain_ref,
+    gain_hbm,
+    vup_hbm,
     wo_hbm,
     wg_hbm,
     wu_hbm,
     wd_hbm,
     out_ref,
+    q_ref,
+    fresh_ref,
+    fresh_all,
+    tables,
+    lengths_ref,
+    rows_ref,
+    order_ref,
+    gain_ref,
+    vup,
+    ring,
+    values,
+    scores,
+    lat,
+    lens,
+    owner_row,
+    owner,
+    ring_sems,
     wo,
     wg,
     wu,
@@ -236,12 +133,23 @@
         local.append(copy)
         return copy
 
-    heads_in = [bring(heads.at[:, :, pl.ds(h * 1024, 1024)], gathered.at[h, g]) for h in range(2)]
-    wo_in = bring(wo_hbm, wo)
-    res_in = bring(residual, res)
-    wg_in = bring(wg_hbm, wg)
-    wu_in = bring(wu_hbm, wu)
-    wd_in = bring(wd_hbm, wd)
+    def piece(i):
+        at = pl.ds(pl.multiple_of(i * PIECE * 128, PIECE * 128), PIECE * 128)
+        at_ring = lax.rem(i, RING)
+        return pltpu.make_async_copy(cache.at[:, at], ring.at[at_ring], ring_sems.at[at_ring])
+
+    tables_in = bring(tables_hbm, tables)
+    small = [
+        bring(queries.at[0], q_ref.at[:, pl.ds(0, HEADS)]),
+        bring(queries.at[1], q_ref.at[:, pl.ds(HEADS, HEADS)]),
+        bring(fresh_hbm, fresh_ref),
+        bring(lengths_hbm, lengths_ref),
+        bring(rows_hbm, rows_ref),
+        bring(order_hbm, order_ref),
+        bring(gain_hbm, gain_ref),
+    ]
+    for i in range(RING):
+        piece(i).start()
 
     barrier = pltpu.get_barrier_semaphore()
     greet = [(group_at(dy, dz), t) for dy, dz in ((1, 0), (-1, 0), (0, 1), (0, -1))]
@@ -250,13 +158,13 @@
         pl.semaphore_signal(barrier, inc=1, device_id=device, device_id_type=MESH)
     pl.semaphore_wait(barrier, len(greet))
 
-    def all_gather(bufs):
+    def all_gather(bufs, cut):
         def slot(h, da, db):
             return group_at(da, db) if h == 0 else group_at(db, da)
 
         def send(h, da, db, to_a, to_b, half=None):
             at = slot(h, da, db)
-            ref = bufs[h].at[at] if half is None else bufs[h].at[at, half]
+            ref = bufs[h].at[at] if half is None else cut(bufs[h], at, half)
             return remote(ref, ref, (slot(h, to_a, to_b), t))
 
         along = [{}, {}]
@@ -276,6 +184,7 @@
             along[h]["+"] = send(h, 0, 0, 1, 0)
             along[h]["-"] = send(h, 0, 0, -1, 0)
             across(h, 0)
+        yield
         for h in range(2):
             along[h]["+"].wait_recv()
             along[h]["++"] = send(h, -1, 0, 1, 0, 0)
@@ -285,13 +194,18 @@
             across(h, 1)
         for h in range(2):
             pass_on(h, 0)
+        yield
         for h in range(2):
             along[h]["++"].wait_recv()
             along[h]["--"].wait_recv()
             across(h, 2)
-        for d in (-1, 1, 2):
+        for d in (-1, 1):
             for h in range(2):
                 pass_on(h, d)
+        yield
+        for h in range(2):
+            pass_on(h, 2)
+        yield
         for d in (0, -1, 1, 2):
             for h in range(2):
                 up2[h][d].wait_recv()
@@ -314,9 +228,24 @@
             total = total + from_x[turn, i].astype(F32)
         return total[:, :COLS]
 
-    for copy in heads_in:
+    tables_in.wait()
+    block_id = lax.broadcasted_iota(jnp.int32, (1, 384), 1)
+
+    def own_blocks(slot, owners):
+        for j in range(BLOCKS):
+            owners = jnp.where(block_id == tables[j, slot], slot, owners)
+        return owners
+
+    owner_row[...] = lax.fori_loop(0, SLOTS, own_blocks, jnp.zeros((1, 384), jnp.int32), unroll=4)
+    owner_in = bring(owner_row, owner)
+    for copy in small:
         copy.wait()
-    all_gather([gathered.at[0], gathered.at[1]])
+    wo_in = bring(wo_hbm, wo)
+    vup_in = bring(vup_hbm, vup)
+    res_in = bring(residual, res)
+    wg_in = bring(wg_hbm, wg)
+    wu_in = bring(wu_hbm, wu)
+    wd_in = bring(wd_hbm, wd)
 
     spread = lax.broadcasted_iota(jnp.int32, (GRPS, GRPS), 1)
     row_of = lax.broadcasted_iota(jnp.int32, (GRPS, GRPS), 0)
@@ -325,21 +254,124 @@
     order = order_ref[...]
     in_group = jnp.logical_and(order >= starts, order < ends)
     group_id = lax.broadcasted_iota(jnp.int32, (GRPS, REQS), 0)
-    at = jnp.sum(jnp.where(in_group, group_id * SLOTS + order - starts, 0), axis=0, keepdims=True)
+    spot = order - starts
+    spot = (spot >> 3) * (GRPS * BATCH) + group_id * BATCH + (spot & 7)
+    at = jnp.sum(jnp.where(in_group, spot, 0), axis=0, keepdims=True)
     matches = lax.broadcasted_iota(jnp.int32, (GRPS * SLOTS, REQS), 0) == at
     select[...] = jnp.where(matches, 1.0, 0.0).astype(BF16)
+    group_row = lax.broadcasted_iota(jnp.int32, (1, GRPS), 1)
+    my_start = jnp.sum(jnp.where(group_row < g, rows_ref[...], 0), axis=1, keepdims=True)
+    my_live = jnp.sum(jnp.where(group_row == g, rows_ref[...], 0), axis=1, keepdims=True)
+    slot_row = lax.broadcasted_iota(jnp.int32, (SLOTS, REQS), 0)
+    named = jnp.logical_and(order - my_start == slot_row, slot_row < my_live)
+    slot_len = jnp.sum(jnp.where(named, lengths_ref[...], 0), axis=1, keepdims=True)
+    lens[...] = jnp.broadcast_to(slot_len, (SLOTS, 128))
+    fresh_all[...] = fresh_ref[...].astype(F32)
+    owner_in.wait()
+
+    lane = lax.broadcasted_iota(jnp.int32, (2 * HEADS, 128), 1)
+
+    def one_piece(i, carry):
+        piece(i).wait()
+        at_ring = lax.rem(i, RING)
+        for c in range(PIECE):
+            chunk = ring[at_ring, :, c * 128 : c * 128 + 128]
+            which = i * PIECE + c
+            both = [
+                q_ref[owner[0, 2 * which + k]] for k in range(2)
+            ]
+            both = jnp.dot(
+                jnp.concatenate(both, axis=0), chunk, preferred_element_type=F32
+            )
+            scores[which] = jnp.where(lane < BLOCK, both[: 2 * HEADS], both[2 * HEADS :])
+            turned = chunk[:RANK, :].T
+            values[2 * which] = turned[:BLOCK]
+            values[2 * which + 1] = turned[BLOCK:]
+
+        @pl.when(i + RING < PIECES)
+        def _():
+            piece(i + RING).start()
+
+        return carry
+
+    lax.fori_loop(0, PIECES, one_piece, 0)
+
+    step_of = lax.broadcasted_iota(jnp.int32, (2 * HEADS, 1), 0) // HEADS
+    PER = 4
+
+    def some_slots(b, it):
+        tiles, picks = [], []
+        for k in range(PER):
+            slot = b * BATCH + it * PER + k
+            q = q_ref[slot].astype(F32)
+            length = lens[pl.ds(slot, 1), :]
+            mine, rows = [], []
+            for j in range(BLOCKS // 2):
+                one, two = tables[2 * j, slot], tables[2 * j + 1, slot]
+                odd_one, odd_two = lax.rem(one, 2), lax.rem(two, 2)
+                two_score = scores[lax.div(two, 2)]
+                two_score = jnp.where(
+                    lane * 0 + odd_one == odd_two, pltpu.roll(two_score, BLOCK, 1), two_score
+                )
+                position = lane + BLOCK * odd_one
+                position = jnp.where(position < 2 * BLOCK, position, position - 2 * BLOCK)
+                tile = jnp.where(position < BLOCK, scores[lax.div(one, 2)], two_score) * score_scale
+                mine.append(jnp.where(position + 128 * j < length, tile, -jnp.inf))
+                rows.append(values[one + (two - one) * odd_one])
+                rows.append(values[two + (one - two) * odd_one])
+            new = [fresh_all[n, pl.ds(slot, 1), :] for n in range(2)]
+            now = jnp.sum(q * new[0], axis=1, keepdims=True) * score_scale
+            later = jnp.sum(q * new[1], axis=1, keepdims=True) * score_scale
+            later = jnp.where(step_of == 1, later, -jnp.inf)
+            tiles.append((jnp.concatenate(mine, axis=1), now, later, new))
+            picks.append(jnp.concatenate(rows, axis=0))
+        for k in range(PER):
+            tile, now, later, new = tiles[k]
+            largest = jnp.maximum(jnp.max(tile, axis=1, keepdims=True), jnp.maximum(now, later))
+            expo = jnp.exp(tile - largest)
+            now = jnp.exp(now - largest)
+            later = jnp.exp(later - largest)
+            inverse = 1.0 / (jnp.sum(expo, axis=1, keepdims=True) + now + later)
+            mixed = jnp.dot(expo.astype(BF16), picks[k], preferred_element_type=F32)
+            mixed = mixed + now * new[0][:, :RANK] + later * new[1][:, :RANK]
+            lat[it * PER + k] = mixed * inverse
+
+    def cut_columns(ref, at, half):
+        return ref.at[at, :, pl.ds(512 * half, 512)]
+
+    running = []
+    for b in range(BATCHES):
+
+        def one_step(it, carry, b=b):
+            some_slots(b, it)
+            return carry
+
+        lax.fori_loop(0, BATCH // PER, one_step, 0)
+        if b == 0:
+            vup_in.wait()
+        for h in range(HEADS):
+            both = jnp.concatenate([lat[:, h, :], lat[:, HEADS + h, :]], axis=0).astype(BF16)
+            value = jnp.dot(both, vup[h], preferred_element_type=F32).astype(BF16)
+            gathered[h // 8, b, g, :, (h % 8) * VH : (h % 8 + 1) * VH] = value
+        running.append(all_gather([gathered.at[h, b] for h in range(2)], cut_columns))
+        for one in running:
+            next(one, None)
 
     wo_in.wait()
     part[:, :, :, :, 384:] = jnp.zeros(part.shape[:-1] + (128,), BF16)
-    TN = (((0,), (0,)), ((), ()))
+    batch_rows = [[], []]
+    for b in range(BATCHES):
+        while next(running[b], True) is None:
+            for one in running[b + 1 :]:
+                next(one, None)
+        both = [gathered[h, b].reshape(GRPS * 2 * BATCH, 1024) for h in range(2)]
+        value = lax.dot_general(both[0], wo[:, :1024], NT, preferred_element_type=F32)
+        value = value + lax.dot_general(both[1], wo[:, 1024:], NT, preferred_element_type=F32)
+        value = value.reshape(GRPS, 2, BATCH, COLS)
+        for s in range(2):
+            batch_rows[s].append(value[:, s].reshape(GRPS * BATCH, COLS).astype(BF16))
     for s in range(2):
-        rows = []
-        for q in range(2):
-            both = [gathered[h, pl.ds(8 * q, 8), s].reshape(8 * SLOTS, 1024) for h in range(2)]
-            value = lax.dot_general(both[0], wo[:, :1024], NT, preferred_element_type=F32)
-            value = value + lax.dot_general(both[1], wo[:, 1024:], NT, preferred_element_type=F32)
-            rows.append(value.astype(BF16))
-        value = jnp.concatenate(rows, axis=0)
+        value = jnp.concatenate(batch_rows[s], axis=0)
         placed = lax.dot_general(select[...], value, TN, preferred_element_type=F32).astype(BF16)
         for k in range(8):
             part[0, k % 2, k // 2, s * 32 : s * 32 + 32, :COLS] = placed[32 * k : 32 * k + 32]
@@ -500,7 +532,8 @@
     for h in range(2):
         for k in range(2):
             hiddens[h, g, k] = hidden[16 * k : 16 * k + 16, 1152 * h : 1152 * h + 1152]
-    all_gather([hiddens.at[0], hiddens.at[1]])
+    for _ in all_gather([hiddens.at[0], hiddens.at[1]], lambda ref, at, half: ref.at[at, half]):
+        pass
 
     wd_in.wait()
     for q in range(4):
@@ -518,22 +551,53 @@
         copy.wait_send()
 
 
-def layer(heads, request_order, group_rows, residual, norm_gain, out_proj, gate_proj, up_proj, down_proj):
-    vmem = pl.BlockSpec(memory_space=pltpu.VMEM)
+def layer(
+    queries,
+    new_latent,
+    latent_cache,
+    tables,
+    context_len,
+    group_rows,
+    request_order,
+    residual,
+    value_up,
+    out_proj,
+    norm_gain,
+    gate_proj,
+    up_proj,
+    down_proj,
+):
     hbm = pl.BlockSpec(memory_space=pl.ANY)
-    copies = 40 + 40 + 4 + 4 + 4 + 3 + 12 + 12
+    copies = BATCHES * 40 + 40 + 4 + 4 + 7 + 12 + 12
     return pl.pallas_call(
         layer_kernel,
         out_shape=jax.ShapeDtypeStruct((2, 32, COLS), BF16),
-        in_specs=[hbm, vmem, vmem, hbm, vmem, hbm, hbm, hbm, hbm],
-        out_specs=vmem,
+        in_specs=[hbm] * 14,
+        out_specs=pl.BlockSpec(memory_space=pltpu.VMEM),
         scratch_shapes=[
+            pltpu.VMEM((SLOTS, 2 * HEADS, KDIM), BF16),
+            pltpu.VMEM((2, SLOTS, KDIM), BF16),
+            pltpu.VMEM((2, SLOTS, KDIM), F32),
+            pltpu.SMEM((BLOCKS, SLOTS), jnp.int32),
+            pltpu.VMEM((1, REQS), jnp.int32),
+            pltpu.VMEM((1, GRPS), jnp.int32),
+            pltpu.VMEM((1, REQS), jnp.int32),
+            pltpu.VMEM((1, COLS), BF16),
+            pltpu.VMEM((HEADS, RANK, VH), BF16),
+            pltpu.VMEM((RING, KDIM, PIECE * 128), BF16),
+            pltpu.VMEM((POOL, BLOCK, RANK), BF16),
+            pltpu.VMEM((POOL // 2, 2 * HEADS, 128), F32),
+            pltpu.VMEM((BATCH, 2 * HEADS, RANK), F32),
+            pltpu.VMEM((SLOTS, 128), jnp.int32),
+            pltpu.VMEM((1, 384), jnp.int32),
+            pltpu.SMEM((1, 384), jnp.int32),
+            pltpu.SemaphoreType.DMA((RING,)),
             pltpu.VMEM((COLS, 2048), BF16),
             pltpu.VMEM((COLS, FFT), BF16),
             pltpu.VMEM((COLS, FFT), BF16),
             pltpu.VMEM((COLS, FFT), BF16),
             pltpu.VMEM((2, COLS, REQS), BF16),
-            pltpu.VMEM((2, GRPS, 2, SLOTS, 1024), BF16),
+            pltpu.VMEM((2, BATCHES, GRPS, 2 * BATCH, 1024), BF16),
             pltpu.VMEM((2, GRPS, 2, 16, 1152), BF16),
             pltpu.VMEM((GRPS * SLOTS, REQS), BF16),
             pltpu.VMEM((64, COLS), F32),
@@ -554,55 +618,28 @@
             pltpu.VMEM((2, 32, 1152), BF16),
             pltpu.VMEM((2, 32, FFT + TAIL), BF16),
             pltpu.VMEM((2, 32, FFT), BF16),
-            pltpu.SemaphoreType.DMA((7,)),
+            pltpu.SemaphoreType.DMA((15,)),
             pltpu.SemaphoreType.DMA((copies,)),
             pltpu.SemaphoreType.DMA((copies,)),
         ],
         compiler_params=pltpu.CompilerParams(
-            collective_id=0, has_side_effects=True, vmem_limit_bytes=56 << 20
+            collective_id=0, has_side_effects=True, vmem_limit_bytes=63 << 20
         ),
     )(
-        heads,
+        queries,
+        new_latent,
+        latent_cache.T,
+        tables.T,
+        context_len.reshape(1, REQS),
+        group_rows.reshape(1, GRPS),
         request_order.reshape(1, REQS),
-        group_rows.reshape(1, GRPS),
         jnp.swapaxes(residual, 1, 2),
         norm_gain.reshape(1, COLS),
+        value_up,
         out_proj.T,
         gate_proj,
         up_proj,
         down_proj.T,
-    )
-
-
-def shards(
-    queries,
-    new_latent,
-    latent_cache,
-    tables,
-    context_len,
-    group_rows,
-    request_order,
-    residual,
-    value_up,
-    out_proj,
-    norm_gain,
-    gate_proj,
-    up_proj,
-    down_proj,
-):
-    heads = attend(
-        queries, new_latent, latent_cache, tables, context_len, group_rows, request_order, value_up
-    )
-    return layer(
-        heads,
-        request_order,
-        group_rows,
-        residual,
-        norm_gain,
-        out_proj,
-        gate_proj,
-        up_proj,
-        down_proj,
     )
 
 
@@ -624,5 +661,5 @@
         P("tp", "grp"),
     )
     return jax.shard_map(
-        shards, mesh=mesh, in_specs=placed, out_specs=P(None, "tp", "grp"), check_vma=False
+        layer, mesh=mesh, in_specs=placed, out_specs=P(None, "tp", "grp"), check_vma=False
     )

time: 157 us -> 137 us (0.87)
  Pallas kernels: 147 us -> 134 us
  local copies, waits for them, and re-layouts: 10.1 us -> 2.73 us
    pallas_call x1 -> x0, Pallas kernels: 26.9 us -> none  [attend(): pl.pallas_call(attention_kernel, out_shape=jax.ShapeDtypeStruct((2, SLOTS...]
    pallas_call x1, Pallas kernels: 120 us -> 134 us  [layer(): pl.pallas_call(layer_kernel, out_shape=jax.ShapeDtypeStruct((2, 32, COLS)...]
    unnamed x16 -> x1, local copies, waits for them, and re-layouts: 8.74 us -> 1.47 us
where the time goes in v3:
time: 137 us
  Pallas kernels  134 us (98%)
  local copies, waits for them, and re-layouts  2.73 us (2%)
    pallas_call x1, Pallas kernels, layer(): pl.pallas_call(layer_kernel, out_shape=jax.ShapeDtypeStruct((2, 32, COLS)...  134 us

profile of v3, /device:TPU:1, one launch (start us, length us, event | category | flops | bytes accessed | tf_op | source)
XLA Modules:
  0.0 136.7 jit_solution(2533533646447587386)
XLA Ops:
  0.0 1.3 reshape.15.gain_hbm
  1.3 134.0 %shard_map.136 = bf16[2,32,448]{2,1,0:T(8,128)(2,1)} custom-call(bf16[2,32,16,576]{3,2,1,0:T(8,128)(2,1)} %queries.1, bf16[2,32,576]{2,1,0:T(8,128)(2,1)} %fresh_hbm.1, bf16[576,20480]{1,0:T(8,128)(2,1)} %bitcast.8, s32[10,32]{1,0:T(8,128)} %bitcast.12, s32[1,256]{1,0:T(1,128)} %bitcast.13, s32[1,16]{1,0:T(1,128)} %bitcast.15, s32[1,256]{1,0:T(1,128)} %bitcast.14, ...), custom_call_target="tpu_custom_call" | custom-call | tf_op jit(solution)/shard_map/pallas_call | solution.py:572
  135.2 1.5 %copy.16 = bf16[2,32,448]{2,1,0:T(8,128)(2,1)} copy(bf16[2,32,448]{2,1,0:T(8,128)(2,1)} %shard_map.136) | data formatting | bytes 114688

commit v4 on v3

--- a/solution.py
+++ b/solution.py
@@ -16,7 +16,7 @@
 GRPS = 16
 REQS = 256
 POOL = 320
-BATCH = 8
+BATCH = 16
 BATCHES = SLOTS // BATCH
 PIECE = 10
 PIECES = POOL // 2 // PIECE
@@ -211,21 +211,25 @@
                 up2[h][d].wait_recv()
                 down2[h][d].wait_recv()
 
-    def scatter_tp(turn):
-        to_core = remote(part.at[turn, 1 - core], from_core.at[turn], (g, partner))
+    def scatter_tp(turn, s):
+        to_core = remote(part.at[turn, s, 1 - core], from_core.at[turn, s], (g, partner))
+        yield
         to_core.wait_recv()
         for k in range(4):
-            summed[turn, k] = (
-                part[turn, core, k].astype(F32) + from_core[turn, k].astype(F32)
+            summed[turn, s, k] = (
+                part[turn, s, core, k].astype(F32) + from_core[turn, s, k].astype(F32)
             ).astype(BF16)
         moves = []
         for i, dx in enumerate((1, -1, 2)):
             chip = lax.rem(x + dx + 4, 4)
-            moves.append(remote(summed.at[turn, chip], from_x.at[turn, i], (g, tp_at(dx))))
-        total = summed[turn, x].astype(F32)
+            moves.append(
+                remote(summed.at[turn, s, chip], from_x.at[turn, s, i], (g, tp_at(dx)))
+            )
+        yield
+        total = summed[turn, s, x].astype(F32)
         for i, move in enumerate(moves):
             move.wait_recv()
-            total = total + from_x[turn, i].astype(F32)
+            total = total + from_x[turn, s, i].astype(F32)
         return total[:, :COLS]
 
     tables_in.wait()
@@ -240,13 +244,6 @@
     owner_in = bring(owner_row, owner)
     for copy in small:
         copy.wait()
-    wo_in = bring(wo_hbm, wo)
-    vup_in = bring(vup_hbm, vup)
-    res_in = bring(residual, res)
-    wg_in = bring(wg_hbm, wg)
-    wu_in = bring(wu_hbm, wu)
-    wd_in = bring(wd_hbm, wd)
-
     spread = lax.broadcasted_iota(jnp.int32, (GRPS, GRPS), 1)
     row_of = lax.broadcasted_iota(jnp.int32, (GRPS, GRPS), 0)
     ends = jnp.sum(jnp.where(spread <= row_of, rows_ref[...], 0), axis=1, keepdims=True)
@@ -255,7 +252,7 @@
     in_group = jnp.logical_and(order >= starts, order < ends)
     group_id = lax.broadcasted_iota(jnp.int32, (GRPS, REQS), 0)
     spot = order - starts
-    spot = (spot >> 3) * (GRPS * BATCH) + group_id * BATCH + (spot & 7)
+    spot = (spot >> 4) * (GRPS * BATCH) + group_id * BATCH + (spot & 15)
     at = jnp.sum(jnp.where(in_group, spot, 0), axis=0, keepdims=True)
     matches = lax.broadcasted_iota(jnp.int32, (GRPS * SLOTS, REQS), 0) == at
     select[...] = jnp.where(matches, 1.0, 0.0).astype(BF16)
@@ -295,6 +292,12 @@
         return carry
 
     lax.fori_loop(0, PIECES, one_piece, 0)
+    vup_in = bring(vup_hbm, vup)
+    wo_in = bring(wo_hbm, wo)
+    res_in = bring(residual, res)
+    wg_in = bring(wg_hbm, wg)
+    wu_in = bring(wu_hbm, wu)
+    wd_in = bring(wd_hbm, wd)
 
     step_of = lax.broadcasted_iota(jnp.int32, (2 * HEADS, 1), 0) // HEADS
     PER = 4
@@ -336,217 +339,269 @@
             mixed = mixed + now * new[0][:, :RANK] + later * new[1][:, :RANK]
             lat[it * PER + k] = mixed * inverse
 
-    def cut_columns(ref, at, half):
+    def cut_heads(ref, at, half):
         return ref.at[at, :, pl.ds(512 * half, 512)]
 
-    running = []
-    for b in range(BATCHES):
-
-        def one_step(it, carry, b=b):
+    def cut_hidden(ref, at, half):
+        return ref.at[at, :, pl.ds(0, 640) if half == 0 else pl.ds(640, 512)]
+
+    part[:, :, :, :, :, 384:] = jnp.zeros(part.shape[:-1] + (128,), BF16)
+    first = (pl.ds(0, 1280), pl.ds(0, 1152))
+    second = (pl.ds(1280, 1152), pl.ds(1152, 1152))
+    rest = pl.ds(0, 1152)
+    chunks, weight = (chunks_a, chunks_b), (wg, wu)
+    relay, final, line = (relay_a, relay_b), (final_a, final_b), (line_a, line_b)
+    relay2, final2 = (relay2_a, relay2_b), (final2_a, final2_b)
+
+    def along(h, d):
+        return (group_at(d, 0) if h == 0 else group_at(0, d), t)
+
+    def across(h, d):
+        return along(1 - h, d)
+
+    def product(s, h):
+        blocks = []
+        for d in range(4):
+            for k in range(4):
+                b = lax.rem(y + d, 4) * 4 + k if h == 0 else k * 4 + lax.rem(z + d, 4)
+                blocks.append(normed[s, b])
+        rows = jnp.concatenate(blocks, axis=0)
+        if h == 0:
+            for d in range(4):
+                chunks[h][s, d, :, FFT:] = rows[64 * d : 64 * d + 64, 384:]
+        rows = rows[:, :COLS]
+        for n in range(3):
+            at = slice(768 * n, 768 * n + 768)
+            value = jnp.dot(rows, weight[h][:, at], preferred_element_type=F32).astype(BF16)
+            for d in range(4):
+                chunks[h][s, d, :, at] = value[64 * d : 64 * d + 64]
+
+    def add(ref, s, index, columns, other):
+        ref[s, index, :, columns] = (
+            ref[s, index, :, columns].astype(F32) + other[...].astype(F32)
+        ).astype(BF16)
+
+    def after_heads(s):
+        if s == 0:
+            wo_in.wait()
+        rows = []
+        for b in range(BATCHES):
+            both = [gathered[h, s, b].reshape(GRPS * BATCH, 1024) for h in range(2)]
+            value = lax.dot_general(both[0], wo[:, :1024], NT, preferred_element_type=F32)
+            value = value + lax.dot_general(both[1], wo[:, 1024:], NT, preferred_element_type=F32)
+            rows.append(value.astype(BF16))
+        value = jnp.concatenate(rows, axis=0)
+        placed = lax.dot_general(select[...], value, TN, preferred_element_type=F32).astype(BF16)
+        for k in range(8):
+            part[0, s, k % 2, k // 2, :, :COLS] = placed[32 * k : 32 * k + 32]
+        attention = yield from scatter_tp(0, s)
+
+        if s == 0:
+            res_in.wait()
+        mine = lax.broadcasted_iota(jnp.int32, (32, REQS), 1) == (
+            lax.broadcasted_iota(jnp.int32, (32, REQS), 0) + t * 32
+        )
+        mine = jnp.where(mine, 1.0, 0.0).astype(BF16)
+        here = lax.dot_general(mine, res[s], NT, preferred_element_type=F32) + attention
+        stream[s] = here
+        squares = jnp.sum(here * here, axis=1, keepdims=True)
+        high = squares.astype(BF16)
+        low = (squares - high.astype(F32)).astype(BF16)
+        extra_lane = lax.broadcasted_iota(jnp.int32, (32, WIDE - COLS), 1)
+        extra = jnp.where(
+            extra_lane == 0, high, jnp.where(extra_lane == 1, low, jnp.zeros_like(high))
+        )
+        scaled = (here * gain_ref[...].astype(F32)).astype(BF16)
+        scaled = jnp.concatenate([scaled, extra], axis=1)
+        normed[s, 2 * t] = scaled[:16]
+        normed[s, 2 * t + 1] = scaled[16:]
+
+        def pair(index):
+            return normed.at[s, pl.ds(2 * index, 2)]
+
+        moves = [remote(pair(t), pair(t), (g, tp_at(dx))) for dx in (1, -1, 2)]
+        moves.append(remote(pair(t), pair(t), (g, partner)))
+        yield
+        shares = []
+        for move, dx in zip(moves[:3], (-1, 1, 2)):
+            move.wait_recv()
+            shares.append(remote(pair(tp_at(dx)), pair(tp_at(dx)), (g, partner)))
+        yield
+        for move in moves[3:] + shares:
+            move.wait_recv()
+        if s == 0:
+            wg_in.wait()
+            wu_in.wait()
+
+        relays, finals, finals2 = [None, None], [[], []], [[], []]
+        for h in range(2):
+            product(s, h)
+            relays[h] = (
+                remote(
+                    chunks[h].at[s, 2, :, first[h]], relay[h].at[s, 0, :, first[h]], along(h, 1)
+                ),
+                remote(chunks[h].at[s, 2, :, second[h]], relay[h].at[s, 1, :, rest], along(h, -1)),
+            )
+            finals[h].append(
+                remote(
+                    chunks[h].at[s, 1, :, second[h]], final[h].at[s, 0, :, second[h]], along(h, 1)
+                )
+            )
+            finals[h].append(
+                remote(
+                    chunks[h].at[s, 3, :, first[h]], final[h].at[s, 1, :, first[h]], along(h, -1)
+                )
+            )
+        yield
+        for h in range(2):
+            relays[h][0].wait_recv()
+            add(chunks[h], s, 1, first[h], relay[h].at[s, 0, :, first[h]])
+            finals[h].append(
+                remote(
+                    chunks[h].at[s, 1, :, first[h]], final[h].at[s, 0, :, first[h]], along(h, 1)
+                )
+            )
+            relays[h][1].wait_recv()
+            add(chunks[h], s, 3, second[h], relay[h].at[s, 1, :, rest])
+            finals[h].append(
+                remote(
+                    chunks[h].at[s, 3, :, second[h]], final[h].at[s, 1, :, second[h]], along(h, -1)
+                )
+            )
+        yield
+        for h in range(2):
+            for copy in finals[h]:
+                copy.wait_recv()
+            for k in range(4):
+                at = pl.ds(16 * k, 16)
+                line[h][s, k] = (
+                    chunks[h][s, 0, at, :].astype(F32)
+                    + final[h][s, 0, at, :].astype(F32)
+                    + final[h][s, 1, at, :].astype(F32)
+                ).astype(BF16)
+            place = z if h == 0 else y
+            far, ahead, behind = [lax.rem(place + d, 4) for d in (2, 1, 3)]
+            relays[h] = (
+                remote(
+                    line[h].at[s, far, :, first[h]], relay2[h].at[s, 0, :, first[h]], across(h, 1)
+                ),
+                remote(
+                    line[h].at[s, far, :, second[h]], relay2[h].at[s, 1, :, rest], across(h, -1)
+                ),
+            )
+            finals2[h].append(
+                remote(
+                    line[h].at[s, ahead, :, second[h]],
+                    final2[h].at[s, 0, :, second[h]],
+                    across(h, 1),
+                )
+            )
+            finals2[h].append(
+                remote(
+                    line[h].at[s, behind, :, first[h]],
+                    final2[h].at[s, 1, :, first[h]],
+                    across(h, -1),
+                )
+            )
+        yield
+        for h in range(2):
+            place = z if h == 0 else y
+            ahead, behind = lax.rem(place + 1, 4), lax.rem(place + 3, 4)
+            relays[h][0].wait_recv()
+            add(line[h], s, ahead, first[h], relay2[h].at[s, 0, :, first[h]])
+            finals2[h].append(
+                remote(
+                    line[h].at[s, ahead, :, first[h]],
+                    final2[h].at[s, 0, :, first[h]],
+                    across(h, 1),
+                )
+            )
+            relays[h][1].wait_recv()
+            add(line[h], s, behind, second[h], relay2[h].at[s, 1, :, rest])
+            finals2[h].append(
+                remote(
+                    line[h].at[s, behind, :, second[h]],
+                    final2[h].at[s, 1, :, second[h]],
+                    across(h, -1),
+                )
+            )
+        yield
+        totals = []
+        for h in range(2):
+            for copy in finals2[h]:
+                copy.wait_recv()
+            place = z if h == 0 else y
+            totals.append(
+                line[h][s, place].astype(F32)
+                + final2[h][s, 0].astype(F32)
+                + final2[h][s, 1].astype(F32)
+            )
+        mean = (totals[0][:, FFT + 64 : FFT + 65] + totals[0][:, FFT + 65 : FFT + 66]) / D
+        inverse_rms = lax.rsqrt(mean + 1e-06)
+        gate = totals[0][:, :FFT] * inverse_rms
+        up = totals[1] * inverse_rms
+        hidden = (gate / (1.0 + jnp.exp(-gate)) * up).astype(BF16)
+        for h in range(2):
+            hiddens[h, s, g] = hidden[:, 1152 * h : 1152 * h + 1152]
+        yield from all_gather([hiddens.at[h, s] for h in range(2)], cut_hidden)
+
+        if s == 0:
+            wd_in.wait()
+        both = [hiddens[h, s].reshape(REQS, 1152) for h in range(2)]
+        value = lax.dot_general(both[0], wd[:, :1152], NT, preferred_element_type=F32)
+        value = value + lax.dot_general(both[1], wd[:, 1152:], NT, preferred_element_type=F32)
+        value = value.astype(BF16)
+        for k in range(8):
+            part[1, s, k % 2, k // 2, :, :COLS] = value[32 * k : 32 * k + 32]
+        reduced = yield from scatter_tp(1, s)
+        out_ref[s] = (stream[s] + reduced).astype(BF16)
+
+    def slots(b, low, high):
+        def one_step(it, carry):
             some_slots(b, it)
             return carry
 
-        lax.fori_loop(0, BATCH // PER, one_step, 0)
-        if b == 0:
-            vup_in.wait()
+        lax.fori_loop(low, high, one_step, 0)
+
+    def raise_values(b):
         for h in range(HEADS):
             both = jnp.concatenate([lat[:, h, :], lat[:, HEADS + h, :]], axis=0).astype(BF16)
             value = jnp.dot(both, vup[h], preferred_element_type=F32).astype(BF16)
-            gathered[h // 8, b, g, :, (h % 8) * VH : (h % 8 + 1) * VH] = value
-        running.append(all_gather([gathered.at[h, b] for h in range(2)], cut_columns))
-        for one in running:
+            for s in range(2):
+                gathered[h // 8, s, b, g, :, (h % 8) * VH : (h % 8 + 1) * VH] = value[
+                    BATCH * s : BATCH * s + BATCH
+                ]
+
+    heads = [
+        [all_gather([gathered.at[h, s, b] for h in range(2)], cut_heads) for b in range(2)]
+        for s in range(2)
+    ]
+    late = [after_heads(s) for s in range(2)]
+
+    def go(*turns):
+        for one in turns:
             next(one, None)
 
-    wo_in.wait()
-    part[:, :, :, :, 384:] = jnp.zeros(part.shape[:-1] + (128,), BF16)
-    batch_rows = [[], []]
-    for b in range(BATCHES):
-        while next(running[b], True) is None:
-            for one in running[b + 1 :]:
-                next(one, None)
-        both = [gathered[h, b].reshape(GRPS * 2 * BATCH, 1024) for h in range(2)]
-        value = lax.dot_general(both[0], wo[:, :1024], NT, preferred_element_type=F32)
-        value = value + lax.dot_general(both[1], wo[:, 1024:], NT, preferred_element_type=F32)
-        value = value.reshape(GRPS, 2, BATCH, COLS)
-        for s in range(2):
-            batch_rows[s].append(value[:, s].reshape(GRPS * BATCH, COLS).astype(BF16))
-    for s in range(2):
-        value = jnp.concatenate(batch_rows[s], axis=0)
-        placed = lax.dot_general(select[...], value, TN, preferred_element_type=F32).astype(BF16)
-        for k in range(8):
-            part[0, k % 2, k // 2, s * 32 : s * 32 + 32, :COLS] = placed[32 * k : 32 * k + 32]
-    attention = scatter_tp(0)
-
-    res_in.wait()
-    mine = lax.broadcasted_iota(jnp.int32, (32, REQS), 1) == (
-        lax.broadcasted_iota(jnp.int32, (32, REQS), 0) + t * 32
-    )
-    mine = jnp.where(mine, 1.0, 0.0).astype(BF16)
-    for s in range(2):
-        own = lax.dot_general(mine, res[s], NT, preferred_element_type=F32)
-        stream[s * 32 : s * 32 + 32, :] = own + attention[s * 32 : s * 32 + 32]
-    here = stream[...]
-    squares = jnp.sum(here * here, axis=1, keepdims=True)
-    high = squares.astype(BF16)
-    low = (squares - high.astype(F32)).astype(BF16)
-    lane = lax.broadcasted_iota(jnp.int32, (64, WIDE - COLS), 1)
-    extra = jnp.where(lane == 0, high, jnp.where(lane == 1, low, jnp.zeros_like(high)))
-    scaled = (here * gain_ref[...].astype(F32)).astype(BF16)
-    scaled = jnp.concatenate([scaled, extra], axis=1)
-    normed[2 * t] = scaled[:32]
-    normed[2 * t + 1] = scaled[32:]
-
-    def pair(index):
-        return normed.at[pl.ds(2 * index, 2)]
-
-    moves = [remote(pair(t), pair(t), (g, tp_at(dx))) for dx in (1, -1, 2)]
-    moves.append(remote(pair(t), pair(t), (g, partner)))
-    shares = []
-    for move, dx in zip(moves[:3], (-1, 1, 2)):
-        move.wait_recv()
-        shares.append(remote(pair(tp_at(dx)), pair(tp_at(dx)), (g, partner)))
-    for move in moves[3:] + shares:
-        move.wait_recv()
-    wg_in.wait()
-    wu_in.wait()
-
-    chunks, weight = (chunks_a, chunks_b), (wg, wu)
-    relay, final, line = (relay_a, relay_b), (final_a, final_b), (line_a, line_b)
-    relay2, final2 = (relay2_a, relay2_b), (final2_a, final2_b)
-    cut = (1280, 1152)
-    first = (pl.ds(0, 1280), pl.ds(0, 1152))
-    second = (pl.ds(1280, 1152), pl.ds(1152, 1152))
-
-    def along(h, d):
-        return (group_at(d, 0) if h == 0 else group_at(0, d), t)
-
-    def across(h, d):
-        return along(1 - h, d)
-
-    def product(h, i, d):
-        blocks = []
-        for k in range(4):
-            b = lax.rem(y + d + 4, 4) * 4 + k if h == 0 else k * 4 + lax.rem(z + d + 4, 4)
-            blocks.append(normed[b])
-        rows = jnp.concatenate(blocks, axis=0)
-        if h == 0:
-            chunks[h][i, :, FFT:] = rows[:, 384:]
-        rows = rows[:, :COLS]
-
-        def one(n, carry):
-            at = pl.ds(pl.multiple_of(n * 256, 256), 256)
-            chunks[h][i, :, at] = jnp.dot(
-                rows, weight[h][:, at], preferred_element_type=F32
-            ).astype(BF16)
-            return carry
-
-        lax.fori_loop(0, FFT // 256, one, 0)
-
-    def add(ref, index, part_cols, other):
-        ref[index, :, part_cols] = (
-            ref[index, :, part_cols].astype(F32) + other[...].astype(F32)
-        ).astype(BF16)
-
-    relays, finals = [None, None], [[], []]
-    for h in range(2):
-        product(h, 2, 2)
-        relays[h] = (
-            remote(chunks[h].at[2, :, first[h]], relay[h].at[0, :, first[h]], along(h, 1)),
-            remote(chunks[h].at[2, :, second[h]], relay[h].at[1, :, pl.ds(0, 1152)], along(h, -1)),
-        )
-    for h in range(2):
-        product(h, 1, 1)
-        finals[h].append(
-            remote(chunks[h].at[1, :, second[h]], final[h].at[0, :, second[h]], along(h, 1))
-        )
-        product(h, 3, -1)
-        finals[h].append(
-            remote(chunks[h].at[3, :, first[h]], final[h].at[1, :, first[h]], along(h, -1))
-        )
-    for h in range(2):
-        relays[h][0].wait_recv()
-        add(chunks[h], 1, first[h], relay[h].at[0, :, first[h]])
-        finals[h].append(
-            remote(chunks[h].at[1, :, first[h]], final[h].at[0, :, first[h]], along(h, 1))
-        )
-        relays[h][1].wait_recv()
-        add(chunks[h], 3, second[h], relay[h].at[1, :, pl.ds(0, 1152)])
-        finals[h].append(
-            remote(chunks[h].at[3, :, second[h]], final[h].at[1, :, second[h]], along(h, -1))
-        )
-    for h in range(2):
-        product(h, 0, 0)
-    relays, finals2 = [None, None], [[], []]
-    for h in range(2):
-        for copy in finals[h]:
-            copy.wait_recv()
-        for k in range(4):
-            at = pl.ds(32 * k, 32)
-            line[h][k] = (
-                chunks[h][0, at, :].astype(F32)
-                + final[h][0, at, :].astype(F32)
-                + final[h][1, at, :].astype(F32)
-            ).astype(BF16)
-        spot = z if h == 0 else y
-
-        def place(d):
-            return lax.rem(spot + d + 4, 4)
-
-        far, ahead, behind = place(2), place(1), place(-1)
-        relays[h] = (
-            remote(line[h].at[far, :, first[h]], relay2[h].at[0, :, first[h]], across(h, 1)),
-            remote(line[h].at[far, :, second[h]], relay2[h].at[1, :, pl.ds(0, 1152)], across(h, -1)),
-        )
-        finals2[h].append(
-            remote(line[h].at[ahead, :, second[h]], final2[h].at[0, :, second[h]], across(h, 1))
-        )
-        finals2[h].append(
-            remote(line[h].at[behind, :, first[h]], final2[h].at[1, :, first[h]], across(h, -1))
-        )
-    totals = []
-    for h in range(2):
-        spot = z if h == 0 else y
-        ahead, behind = lax.rem(spot + 1, 4), lax.rem(spot + 3, 4)
-        relays[h][0].wait_recv()
-        add(line[h], ahead, first[h], relay2[h].at[0, :, first[h]])
-        finals2[h].append(
-            remote(line[h].at[ahead, :, first[h]], final2[h].at[0, :, first[h]], across(h, 1))
-        )
-        relays[h][1].wait_recv()
-        add(line[h], behind, second[h], relay2[h].at[1, :, pl.ds(0, 1152)])
-        finals2[h].append(
-            remote(line[h].at[behind, :, second[h]], final2[h].at[1, :, second[h]], across(h, -1))
-        )
-    for h in range(2):
-        for copy in finals2[h]:
-            copy.wait_recv()
-        spot = z if h == 0 else y
-        totals.append(
-            line[h][spot].astype(F32) + final2[h][0].astype(F32) + final2[h][1].astype(F32)
-        )
-    mean = (totals[0][:, FFT + 64 : FFT + 65] + totals[0][:, FFT + 65 : FFT + 66]) / D
-    inverse_rms = lax.rsqrt(mean + 1e-06)
-    gate = totals[0][:, :FFT] * inverse_rms
-    up = totals[1] * inverse_rms
-    hidden = (gate / (1.0 + jnp.exp(-gate)) * up).astype(BF16)
-    for h in range(2):
-        for k in range(2):
-            hiddens[h, g, k] = hidden[16 * k : 16 * k + 16, 1152 * h : 1152 * h + 1152]
-    for _ in all_gather([hiddens.at[0], hiddens.at[1]], lambda ref, at, half: ref.at[at, half]):
-        pass
-
-    wd_in.wait()
-    for q in range(4):
-        both = [hiddens[h, 4 * q : 4 * q + 4].reshape(128, 1152) for h in range(2)]
-        value = lax.dot_general(both[0], wd[:, :1152], NT, preferred_element_type=F32)
-        value = value + lax.dot_general(both[1], wd[:, 1152:], NT, preferred_element_type=F32)
-        value = value.astype(BF16)
-        for k in range(2):
-            part[1, k, q, :, :COLS] = value[64 * k : 64 * k + 64]
-    reduced = scatter_tp(1)
-    for s in range(2):
-        at = slice(32 * s, 32 * s + 32)
-        out_ref[s] = (stream[at, :] + reduced[at]).astype(BF16)
+    slots(0, 0, 4)
+    vup_in.wait()
+    raise_values(0)
+    go(heads[0][0])
+    slots(1, 0, 2)
+    go(heads[0][0])
+    slots(1, 2, 4)
+    raise_values(1)
+    go(heads[0][1], heads[0][0])
+    go(heads[1][0], heads[0][1], heads[0][0])
+    go(heads[0][1], heads[0][0], heads[1][1])
+    go(heads[0][1], heads[1][0], heads[0][1])
+    go(late[0], heads[1][0], heads[1][1])
+    go(late[0], heads[1][0], heads[1][1])
+    go(late[0], heads[1][0], heads[1][1])
+    go(late[0], late[0], heads[1][1])
+    go(late[1], late[0], late[1], late[1], late[1], late[1])
+    for _ in range(9):
+        go(late[0], late[1])
+    go(late[1])
     for copy in used:
         copy.wait_send()
 
@@ -568,7 +623,7 @@
     down_proj,
 ):
     hbm = pl.BlockSpec(memory_space=pl.ANY)
-    copies = BATCHES * 40 + 40 + 4 + 4 + 7 + 12 + 12
+    copies = 4 * 40 + 2 * 40 + 4 * 4 + 2 * 7 + 2 * 24
     return pl.pallas_call(
         layer_kernel,
         out_shape=jax.ShapeDtypeStruct((2, 32, COLS), BF16),
@@ -597,27 +652,27 @@
             pltpu.VMEM((COLS, FFT), BF16),
             pltpu.VMEM((COLS, FFT), BF16),
             pltpu.VMEM((2, COLS, REQS), BF16),
-            pltpu.VMEM((2, BATCHES, GRPS, 2 * BATCH, 1024), BF16),
-            pltpu.VMEM((2, GRPS, 2, 16, 1152), BF16),
+            pltpu.VMEM((2, 2, BATCHES, GRPS, BATCH, 1024), BF16),
+            pltpu.VMEM((2, 2, GRPS, 16, 1152), BF16),
             pltpu.VMEM((GRPS * SLOTS, REQS), BF16),
-            pltpu.VMEM((64, COLS), F32),
-            pltpu.VMEM((2, 2, 4, 64, WIDE), BF16),
-            pltpu.VMEM((2, 4, 64, WIDE), BF16),
-            pltpu.VMEM((2, 4, 64, WIDE), BF16),
-            pltpu.VMEM((2, 3, 64, WIDE), BF16),
-            pltpu.VMEM((16, 32, WIDE), BF16),
-            pltpu.VMEM((4, 128, FFT + TAIL), BF16),
-            pltpu.VMEM((4, 128, FFT), BF16),
-            pltpu.VMEM((2, 128, 1280), BF16),
-            pltpu.VMEM((2, 128, 1152), BF16),
-            pltpu.VMEM((2, 128, FFT + TAIL), BF16),
-            pltpu.VMEM((2, 128, FFT), BF16),
-            pltpu.VMEM((4, 32, FFT + TAIL), BF16),
-            pltpu.VMEM((4, 32, FFT), BF16),
-            pltpu.VMEM((2, 32, 1280), BF16),
-            pltpu.VMEM((2, 32, 1152), BF16),
-            pltpu.VMEM((2, 32, FFT + TAIL), BF16),
-            pltpu.VMEM((2, 32, FFT), BF16),
+            pltpu.VMEM((2, 32, COLS), F32),
+            pltpu.VMEM((2, 2, 2, 4, 32, WIDE), BF16),
+            pltpu.VMEM((2, 2, 4, 32, WIDE), BF16),
+            pltpu.VMEM((2, 2, 4, 32, WIDE), BF16),
+            pltpu.VMEM((2, 2, 3, 32, WIDE), BF16),
+            pltpu.VMEM((2, 16, 16, WIDE), BF16),
+            pltpu.VMEM((2, 4, 64, FFT + TAIL), BF16),
+            pltpu.VMEM((2, 4, 64, FFT), BF16),
+            pltpu.VMEM((2, 2, 64, 1280), BF16),
+            pltpu.VMEM((2, 2, 64, 1152), BF16),
+            pltpu.VMEM((2, 2, 64, FFT + TAIL), BF16),
+            pltpu.VMEM((2, 2, 64, FFT), BF16),
+            pltpu.VMEM((2, 4, 16, FFT + TAIL), BF16),
+            pltpu.VMEM((2, 4, 16, FFT), BF16),
+            pltpu.VMEM((2, 2, 16, 1280), BF16),
+            pltpu.VMEM((2, 2, 16, 1152), BF16),
+            pltpu.VMEM((2, 2, 16, FFT + TAIL), BF16),
+            pltpu.VMEM((2, 2, 16, FFT), BF16),
             pltpu.SemaphoreType.DMA((15,)),
             pltpu.SemaphoreType.DMA((copies,)),
             pltpu.SemaphoreType.DMA((copies,)),

time: 137 us -> 126 us (0.920)
  Pallas kernels: 134 us -> 123 us
    pallas_call x1, Pallas kernels: 134 us -> 123 us  [layer(): pl.pallas_call(layer_kernel, out_shape=jax.ShapeDtypeStruct((2, 32, COLS)...]
where the time goes in v4:
time: 126 us
  Pallas kernels  123 us (98%)
  local copies, waits for them, and re-layouts  2.73 us (2%)
    pallas_call x1, Pallas kernels, layer(): pl.pallas_call(layer_kernel, out_shape=jax.ShapeDtypeStruct((2, 32, COLS)...  123 us

profile of v4, /device:TPU:1, one launch (start us, length us, event | category | flops | bytes accessed | tf_op | source)
XLA Modules:
  0.0 126.2 jit_solution(8274067676284735228)
XLA Ops:
  0.0 1.3 reshape.15.gain_hbm
  1.3 123.5 %shard_map.136 = bf16[2,32,448]{2,1,0:T(8,128)(2,1)} custom-call(bf16[2,32,16,576]{3,2,1,0:T(8,128)(2,1)} %queries.1, bf16[2,32,576]{2,1,0:T(8,128)(2,1)} %fresh_hbm.1, bf16[576,20480]{1,0:T(8,128)(2,1)} %bitcast.8, s32[10,32]{1,0:T(8,128)} %bitcast.12, s32[1,256]{1,0:T(1,128)} %bitcast.13, s32[1,16]{1,0:T(1,128)} %bitcast.15, s32[1,256]{1,0:T(1,128)} %bitcast.14, ...), custom_call_target="tpu_custom_call" | custom-call | tf_op jit(solution)/shard_map/pallas_call | solution.py:627
  124.7 1.5 %copy.16 = bf16[2,32,448]{2,1,0:T(8,128)(2,1)} copy(bf16[2,32,448]{2,1,0:T(8,128)(2,1)} %shard_map.136) | data formatting | bytes 114688

commit v5 on v4

--- a/solution.py
+++ b/solution.py
@@ -20,7 +20,7 @@
 BATCHES = SLOTS // BATCH
 PIECE = 10
 PIECES = POOL // 2 // PIECE
-RING = 3
+RING = 4
 
 score_scale = 192.0 ** (-0.5)
 NT = (((1,), (1,)), ((), ()))
@@ -68,10 +68,8 @@
     owner_row,
     owner,
     ring_sems,
-    wo,
     wg,
     wu,
-    wd,
     res,
     gathered,
     hiddens,
@@ -79,7 +77,6 @@
     stream,
     part,
     from_core,
-    summed,
     from_x,
     normed,
     chunks_a,
@@ -90,8 +87,6 @@
     final_b,
     line_a,
     line_b,
-    relay2_a,
-    relay2_b,
     final2_a,
     final2_b,
     local_sems,
@@ -139,24 +134,25 @@
         return pltpu.make_async_copy(cache.at[:, at], ring.at[at_ring], ring_sems.at[at_ring])
 
     tables_in = bring(tables_hbm, tables)
-    small = [
+    queries_in = [
         bring(queries.at[0], q_ref.at[:, pl.ds(0, HEADS)]),
         bring(queries.at[1], q_ref.at[:, pl.ds(HEADS, HEADS)]),
+    ]
+    for i in range(RING):
+        piece(i).start()
+    small = [
         bring(fresh_hbm, fresh_ref),
         bring(lengths_hbm, lengths_ref),
         bring(rows_hbm, rows_ref),
         bring(order_hbm, order_ref),
         bring(gain_hbm, gain_ref),
     ]
-    for i in range(RING):
-        piece(i).start()
 
     barrier = pltpu.get_barrier_semaphore()
-    greet = [(group_at(dy, dz), t) for dy, dz in ((1, 0), (-1, 0), (0, 1), (0, -1))]
+    greet = [(group_at(dy, dz), t) for dy, dz in ((1, 0), (-1, 0), (2, 0), (0, 1), (0, -1), (0, 2))]
     greet += [(g, tp_at(1)), (g, tp_at(-1)), (g, tp_at(2)), (g, partner)]
     for device in greet:
         pl.semaphore_signal(barrier, inc=1, device_id=device, device_id_type=MESH)
-    pl.semaphore_wait(barrier, len(greet))
 
     def all_gather(bufs, cut):
         def slot(h, da, db):
@@ -181,30 +177,24 @@
             down2[h][d] = send(h, d, 1, 0, -1, 1)
 
         for h in range(2):
-            along[h]["+"] = send(h, 0, 0, 1, 0)
-            along[h]["-"] = send(h, 0, 0, -1, 0)
+            along[h][-1] = send(h, 0, 0, 1, 0)
+            along[h][1] = send(h, 0, 0, -1, 0)
             across(h, 0)
-        yield
-        for h in range(2):
-            along[h]["+"].wait_recv()
-            along[h]["++"] = send(h, -1, 0, 1, 0, 0)
-            across(h, -1)
-            along[h]["-"].wait_recv()
-            along[h]["--"] = send(h, 1, 0, -1, 0, 1)
-            across(h, 1)
-        for h in range(2):
-            pass_on(h, 0)
-        yield
-        for h in range(2):
-            along[h]["++"].wait_recv()
-            along[h]["--"].wait_recv()
-            across(h, 2)
+            along[h][2] = send(h, 0, 0, 2, 0)
+        yield
         for d in (-1, 1):
             for h in range(2):
+                along[h][d].wait_recv()
+                across(h, d)
+        for h in range(2):
+            pass_on(h, 0)
+        for h in range(2):
+            along[h][2].wait_recv()
+            across(h, 2)
+        yield
+        for d in (-1, 1, 2):
+            for h in range(2):
                 pass_on(h, d)
-        yield
-        for h in range(2):
-            pass_on(h, 2)
         yield
         for d in (0, -1, 1, 2):
             for h in range(2):
@@ -216,17 +206,17 @@
         yield
         to_core.wait_recv()
         for k in range(4):
-            summed[turn, s, k] = (
+            part[turn, s, core, k] = (
                 part[turn, s, core, k].astype(F32) + from_core[turn, s, k].astype(F32)
             ).astype(BF16)
         moves = []
         for i, dx in enumerate((1, -1, 2)):
             chip = lax.rem(x + dx + 4, 4)
             moves.append(
-                remote(summed.at[turn, s, chip], from_x.at[turn, s, i], (g, tp_at(dx)))
-            )
-        yield
-        total = summed[turn, s, x].astype(F32)
+                remote(part.at[turn, s, core, chip], from_x.at[turn, s, i], (g, tp_at(dx)))
+            )
+        yield
+        total = part[turn, s, core, x].astype(F32)
         for i, move in enumerate(moves):
             move.wait_recv()
             total = total + from_x[turn, s, i].astype(F32)
@@ -242,6 +232,45 @@
 
     owner_row[...] = lax.fori_loop(0, SLOTS, own_blocks, jnp.zeros((1, 384), jnp.int32), unroll=4)
     owner_in = bring(owner_row, owner)
+    for copy in queries_in:
+        copy.wait()
+    owner_in.wait()
+
+    lane = lax.broadcasted_iota(jnp.int32, (2 * HEADS, 128), 1)
+
+    def one_piece(i, carry):
+        piece(i).wait()
+        at_ring = lax.rem(i, RING)
+        for c in range(PIECE):
+            chunk = ring[at_ring, :, c * 128 : c * 128 + 128]
+            which = i * PIECE + c
+            both = [
+                q_ref[owner[0, 2 * which + k]] for k in range(2)
+            ]
+            both = jnp.dot(
+                jnp.concatenate(both, axis=0), chunk, preferred_element_type=F32
+            )
+            scores[which] = jnp.where(lane < BLOCK, both[: 2 * HEADS], both[2 * HEADS :])
+            turned = chunk[:RANK, :].T
+            values[2 * which] = turned[:BLOCK]
+            values[2 * which + 1] = turned[BLOCK:]
+
+        @pl.when(i + RING < PIECES)
+        def _():
+            piece(i + RING).start()
+
+        return carry
+
+    lax.fori_loop(0, PIECES, one_piece, 0)
+    vup_in = bring(vup_hbm, vup)
+    wo = [ring.at[2 + h, pl.ds(0, COLS), pl.ds(0, 1024)] for h in range(2)]
+    wo_in = [bring(wo_hbm.at[:, pl.ds(1024 * h, 1024)], wo[h]) for h in range(2)]
+    res_in = bring(residual, res)
+    wg_in = bring(wg_hbm, wg)
+    wu_in = bring(wu_hbm, wu)
+    wd = [ring.at[h, pl.ds(0, COLS), pl.ds(0, 1152)] for h in range(2)]
+    wd_in = [bring(wd_hbm.at[:, pl.ds(1152 * h, 1152)], wd[h]) for h in range(2)]
+
     for copy in small:
         copy.wait()
     spread = lax.broadcasted_iota(jnp.int32, (GRPS, GRPS), 1)
@@ -264,40 +293,6 @@
     slot_len = jnp.sum(jnp.where(named, lengths_ref[...], 0), axis=1, keepdims=True)
     lens[...] = jnp.broadcast_to(slot_len, (SLOTS, 128))
     fresh_all[...] = fresh_ref[...].astype(F32)
-    owner_in.wait()
-
-    lane = lax.broadcasted_iota(jnp.int32, (2 * HEADS, 128), 1)
-
-    def one_piece(i, carry):
-        piece(i).wait()
-        at_ring = lax.rem(i, RING)
-        for c in range(PIECE):
-            chunk = ring[at_ring, :, c * 128 : c * 128 + 128]
-            which = i * PIECE + c
-            both = [
-                q_ref[owner[0, 2 * which + k]] for k in range(2)
-            ]
-            both = jnp.dot(
-                jnp.concatenate(both, axis=0), chunk, preferred_element_type=F32
-            )
-            scores[which] = jnp.where(lane < BLOCK, both[: 2 * HEADS], both[2 * HEADS :])
-            turned = chunk[:RANK, :].T
-            values[2 * which] = turned[:BLOCK]
-            values[2 * which + 1] = turned[BLOCK:]
-
-        @pl.when(i + RING < PIECES)
-        def _():
-            piece(i + RING).start()
-
-        return carry
-
-    lax.fori_loop(0, PIECES, one_piece, 0)
-    vup_in = bring(vup_hbm, vup)
-    wo_in = bring(wo_hbm, wo)
-    res_in = bring(residual, res)
-    wg_in = bring(wg_hbm, wg)
-    wu_in = bring(wu_hbm, wu)
-    wd_in = bring(wd_hbm, wd)
 
     step_of = lax.broadcasted_iota(jnp.int32, (2 * HEADS, 1), 0) // HEADS
     PER = 4
@@ -351,7 +346,7 @@
     rest = pl.ds(0, 1152)
     chunks, weight = (chunks_a, chunks_b), (wg, wu)
     relay, final, line = (relay_a, relay_b), (final_a, final_b), (line_a, line_b)
-    relay2, final2 = (relay2_a, relay2_b), (final2_a, final2_b)
+    final2 = (final2_a, final2_b)
 
     def along(h, d):
         return (group_at(d, 0) if h == 0 else group_at(0, d), t)
@@ -383,12 +378,13 @@
 
     def after_heads(s):
         if s == 0:
-            wo_in.wait()
+            for copy in wo_in:
+                copy.wait()
         rows = []
         for b in range(BATCHES):
             both = [gathered[h, s, b].reshape(GRPS * BATCH, 1024) for h in range(2)]
-            value = lax.dot_general(both[0], wo[:, :1024], NT, preferred_element_type=F32)
-            value = value + lax.dot_general(both[1], wo[:, 1024:], NT, preferred_element_type=F32)
+            value = lax.dot_general(both[0], wo[0][...], NT, preferred_element_type=F32)
+            value = value + lax.dot_general(both[1], wo[1][...], NT, preferred_element_type=F32)
             rows.append(value.astype(BF16))
         value = jnp.concatenate(rows, axis=0)
         placed = lax.dot_general(select[...], value, TN, preferred_element_type=F32).astype(BF16)
@@ -411,7 +407,7 @@
         extra = jnp.where(
             extra_lane == 0, high, jnp.where(extra_lane == 1, low, jnp.zeros_like(high))
         )
-        scaled = (here * gain_ref[...].astype(F32)).astype(BF16)
+        scaled = (here * gain_ref[...].reshape(1, COLS).astype(F32)).astype(BF16)
         scaled = jnp.concatenate([scaled, extra], axis=1)
         normed[s, 2 * t] = scaled[:16]
         normed[s, 2 * t + 1] = scaled[16:]
@@ -480,51 +476,9 @@
                     + final[h][s, 1, at, :].astype(F32)
                 ).astype(BF16)
             place = z if h == 0 else y
-            far, ahead, behind = [lax.rem(place + d, 4) for d in (2, 1, 3)]
-            relays[h] = (
-                remote(
-                    line[h].at[s, far, :, first[h]], relay2[h].at[s, 0, :, first[h]], across(h, 1)
-                ),
-                remote(
-                    line[h].at[s, far, :, second[h]], relay2[h].at[s, 1, :, rest], across(h, -1)
-                ),
-            )
-            finals2[h].append(
-                remote(
-                    line[h].at[s, ahead, :, second[h]],
-                    final2[h].at[s, 0, :, second[h]],
-                    across(h, 1),
-                )
-            )
-            finals2[h].append(
-                remote(
-                    line[h].at[s, behind, :, first[h]],
-                    final2[h].at[s, 1, :, first[h]],
-                    across(h, -1),
-                )
-            )
-        yield
-        for h in range(2):
-            place = z if h == 0 else y
-            ahead, behind = lax.rem(place + 1, 4), lax.rem(place + 3, 4)
-            relays[h][0].wait_recv()
-            add(line[h], s, ahead, first[h], relay2[h].at[s, 0, :, first[h]])
-            finals2[h].append(
-                remote(
-                    line[h].at[s, ahead, :, first[h]],
-                    final2[h].at[s, 0, :, first[h]],
-                    across(h, 1),
-                )
-            )
-            relays[h][1].wait_recv()
-            add(line[h], s, behind, second[h], relay2[h].at[s, 1, :, rest])
-            finals2[h].append(
-                remote(
-                    line[h].at[s, behind, :, second[h]],
-                    final2[h].at[s, 1, :, second[h]],
-                    across(h, -1),
-                )
-            )
+            for i, d in enumerate((1, -1, 2)):
+                block = line[h].at[s, lax.rem(place + d + 4, 4)]
+                finals2[h].append(remote(block, final2[h].at[s, i], across(h, d)))
         yield
         totals = []
         for h in range(2):
@@ -535,6 +489,7 @@
                 line[h][s, place].astype(F32)
                 + final2[h][s, 0].astype(F32)
                 + final2[h][s, 1].astype(F32)
+                + final2[h][s, 2].astype(F32)
             )
         mean = (totals[0][:, FFT + 64 : FFT + 65] + totals[0][:, FFT + 65 : FFT + 66]) / D
         inverse_rms = lax.rsqrt(mean + 1e-06)
@@ -546,10 +501,11 @@
         yield from all_gather([hiddens.at[h, s] for h in range(2)], cut_hidden)
 
         if s == 0:
-            wd_in.wait()
+            for copy in wd_in:
+                copy.wait()
         both = [hiddens[h, s].reshape(REQS, 1152) for h in range(2)]
-        value = lax.dot_general(both[0], wd[:, :1152], NT, preferred_element_type=F32)
-        value = value + lax.dot_general(both[1], wd[:, 1152:], NT, preferred_element_type=F32)
+        value = lax.dot_general(both[0], wd[0][...], NT, preferred_element_type=F32)
+        value = value + lax.dot_general(both[1], wd[1][...], NT, preferred_element_type=F32)
         value = value.astype(BF16)
         for k in range(8):
             part[1, s, k % 2, k // 2, :, :COLS] = value[32 * k : 32 * k + 32]
@@ -585,21 +541,24 @@
     slots(0, 0, 4)
     vup_in.wait()
     raise_values(0)
+    pl.semaphore_wait(barrier, len(greet))
     go(heads[0][0])
-    slots(1, 0, 2)
+    slots(1, 0, 1)
+    go(heads[1][0])
+    slots(1, 1, 2)
     go(heads[0][0])
-    slots(1, 2, 4)
+    slots(1, 2, 3)
+    go(heads[1][0])
+    slots(1, 3, 4)
     raise_values(1)
-    go(heads[0][1], heads[0][0])
-    go(heads[1][0], heads[0][1], heads[0][0])
-    go(heads[0][1], heads[0][0], heads[1][1])
+    go(heads[0][1], heads[0][0], heads[0][1], heads[1][1], heads[0][0])
     go(heads[0][1], heads[1][0], heads[0][1])
-    go(late[0], heads[1][0], heads[1][1])
-    go(late[0], heads[1][0], heads[1][1])
-    go(late[0], heads[1][0], heads[1][1])
-    go(late[0], late[0], heads[1][1])
+    go(late[0], heads[1][1], heads[1][0])
+    go(late[0], heads[1][1])
+    go(late[0], heads[1][1])
+    go(late[0], late[0])
     go(late[1], late[0], late[1], late[1], late[1], late[1])
-    for _ in range(9):
+    for _ in range(7):
         go(late[0], late[1])
     go(late[1])
     for copy in used:
@@ -623,7 +582,7 @@
     down_proj,
 ):
     hbm = pl.BlockSpec(memory_space=pl.ANY)
-    copies = 4 * 40 + 2 * 40 + 4 * 4 + 2 * 7 + 2 * 24
+    copies = 4 * 38 + 2 * 38 + 4 * 4 + 2 * 7 + 2 * 18
     return pl.pallas_call(
         layer_kernel,
         out_shape=jax.ShapeDtypeStruct((2, 32, COLS), BF16),
@@ -637,7 +596,7 @@
             pltpu.VMEM((1, REQS), jnp.int32),
             pltpu.VMEM((1, GRPS), jnp.int32),
             pltpu.VMEM((1, REQS), jnp.int32),
-            pltpu.VMEM((1, COLS), BF16),
+            pltpu.VMEM((COLS,), BF16),
             pltpu.VMEM((HEADS, RANK, VH), BF16),
             pltpu.VMEM((RING, KDIM, PIECE * 128), BF16),
             pltpu.VMEM((POOL, BLOCK, RANK), BF16),
@@ -647,8 +606,6 @@
             pltpu.VMEM((1, 384), jnp.int32),
             pltpu.SMEM((1, 384), jnp.int32),
             pltpu.SemaphoreType.DMA((RING,)),
-            pltpu.VMEM((COLS, 2048), BF16),
-            pltpu.VMEM((COLS, FFT), BF16),
             pltpu.VMEM((COLS, FFT), BF16),
             pltpu.VMEM((COLS, FFT), BF16),
             pltpu.VMEM((2, COLS, REQS), BF16),
@@ -657,7 +614,6 @@
             pltpu.VMEM((GRPS * SLOTS, REQS), BF16),
             pltpu.VMEM((2, 32, COLS), F32),
             pltpu.VMEM((2, 2, 2, 4, 32, WIDE), BF16),
-            pltpu.VMEM((2, 2, 4, 32, WIDE), BF16),
             pltpu.VMEM((2, 2, 4, 32, WIDE), BF16),
             pltpu.VMEM((2, 2, 3, 32, WIDE), BF16),
             pltpu.VMEM((2, 16, 16, WIDE), BF16),
@@ -669,11 +625,9 @@
             pltpu.VMEM((2, 2, 64, FFT), BF16),
             pltpu.VMEM((2, 4, 16, FFT + TAIL), BF16),
             pltpu.VMEM((2, 4, 16, FFT), BF16),
-            pltpu.VMEM((2, 2, 16, 1280), BF16),
-            pltpu.VMEM((2, 2, 16, 1152), BF16),
-            pltpu.VMEM((2, 2, 16, FFT + TAIL), BF16),
-            pltpu.VMEM((2, 2, 16, FFT), BF16),
-            pltpu.SemaphoreType.DMA((15,)),
+            pltpu.VMEM((2, 3, 16, FFT + TAIL), BF16),
+            pltpu.VMEM((2, 3, 16, FFT), BF16),
+            pltpu.SemaphoreType.DMA((17,)),
             pltpu.SemaphoreType.DMA((copies,)),
             pltpu.SemaphoreType.DMA((copies,)),
         ],
@@ -689,7 +643,7 @@
         group_rows.reshape(1, GRPS),
         request_order.reshape(1, REQS),
         jnp.swapaxes(residual, 1, 2),
-        norm_gain.reshape(1, COLS),
+        norm_gain,
         value_up,
         out_proj.T,
         gate_proj,

time: 126 us -> 121 us (0.960)
  Pallas kernels: 123 us -> 119 us
  local copies, waits for them, and re-layouts: 2.73 us -> 1.47 us
    pallas_call x1, Pallas kernels: 123 us -> 119 us  [layer(): pl.pallas_call(layer_kernel, out_shape=jax.ShapeDtypeStruct((2, 32, COLS)...]
where the time goes in v5:
time: 121 us; the launch traced here: 120 us
  Pallas kernels  119 us (98%)
  local copies, waits for them, and re-layouts  1.47 us (1%)
    pallas_call x1, Pallas kernels, layer(): pl.pallas_call(layer_kernel, out_shape=jax.ShapeDtypeStruct((2, 32, COLS)...  119 us

profile of v5, /device:TPU:1, one launch (start us, length us, event | category | flops | bytes accessed | tf_op | source)
XLA Modules:
  0.0 120.5 jit_solution(10717586142994894656)
XLA Ops:
  0.0 119.0 %shard_map.136 = bf16[2,32,448]{2,1,0:T(8,128)(2,1)} custom-call(bf16[2,32,16,576]{3,2,1,0:T(8,128)(2,1)} %queries.1, bf16[2,32,576]{2,1,0:T(8,128)(2,1)} %fresh_hbm.1, bf16[576,20480]{1,0:T(8,128)(2,1)} %bitcast.8, s32[10,32]{1,0:T(8,128)} %bitcast.12, s32[1,256]{1,0:T(1,128)} %bitcast.13, s32[1,16]{1,0:T(1,128)} %bitcast.15, s32[1,256]{1,0:T(1,128)} %bitcast.14, ...), custom_call_target="tpu_custom_call" | custom-call | tf_op jit(solution)/shard_map/pallas_call | solution.py:586
  119.0 1.5 %copy.16 = bf16[2,32,448]{2,1,0:T(8,128)(2,1)} copy(bf16[2,32,448]{2,1,0:T(8,128)(2,1)} %shard_map.136) | data formatting | bytes 114688

commit v6 on v5

--- a/solution.py
+++ b/solution.py
@@ -273,18 +273,7 @@
 
     for copy in small:
         copy.wait()
-    spread = lax.broadcasted_iota(jnp.int32, (GRPS, GRPS), 1)
-    row_of = lax.broadcasted_iota(jnp.int32, (GRPS, GRPS), 0)
-    ends = jnp.sum(jnp.where(spread <= row_of, rows_ref[...], 0), axis=1, keepdims=True)
-    starts = jnp.sum(jnp.where(spread < row_of, rows_ref[...], 0), axis=1, keepdims=True)
     order = order_ref[...]
-    in_group = jnp.logical_and(order >= starts, order < ends)
-    group_id = lax.broadcasted_iota(jnp.int32, (GRPS, REQS), 0)
-    spot = order - starts
-    spot = (spot >> 4) * (GRPS * BATCH) + group_id * BATCH + (spot & 15)
-    at = jnp.sum(jnp.where(in_group, spot, 0), axis=0, keepdims=True)
-    matches = lax.broadcasted_iota(jnp.int32, (GRPS * SLOTS, REQS), 0) == at
-    select[...] = jnp.where(matches, 1.0, 0.0).astype(BF16)
     group_row = lax.broadcasted_iota(jnp.int32, (1, GRPS), 1)
     my_start = jnp.sum(jnp.where(group_row < g, rows_ref[...], 0), axis=1, keepdims=True)
     my_live = jnp.sum(jnp.where(group_row == g, rows_ref[...], 0), axis=1, keepdims=True)
@@ -552,6 +541,17 @@
     slots(1, 3, 4)
     raise_values(1)
     go(heads[0][1], heads[0][0], heads[0][1], heads[1][1], heads[0][0])
+    spread = lax.broadcasted_iota(jnp.int32, (GRPS, GRPS), 1)
+    row_of = lax.broadcasted_iota(jnp.int32, (GRPS, GRPS), 0)
+    ends = jnp.sum(jnp.where(spread <= row_of, rows_ref[...], 0), axis=1, keepdims=True)
+    starts = jnp.sum(jnp.where(spread < row_of, rows_ref[...], 0), axis=1, keepdims=True)
+    in_group = jnp.logical_and(order >= starts, order < ends)
+    group_id = lax.broadcasted_iota(jnp.int32, (GRPS, REQS), 0)
+    spot = order - starts
+    spot = (spot >> 4) * (GRPS * BATCH) + group_id * BATCH + (spot & 15)
+    at = jnp.sum(jnp.where(in_group, spot, 0), axis=0, keepdims=True)
+    matches = lax.broadcasted_iota(jnp.int32, (GRPS * SLOTS, REQS), 0) == at
+    select[...] = jnp.where(matches, 1.0, 0.0).astype(BF16)
     go(heads[0][1], heads[1][0], heads[0][1])
     go(late[0], heads[1][1], heads[1][0])
     go(late[0], heads[1][1])

time: 121 us -> 121 us (level)
  no operation moved by 1% of the time
where the time goes in v6:
time: 121 us
  Pallas kernels  120 us (99%)
  local copies, waits for them, and re-layouts  1.47 us (1%)
    pallas_call x1, Pallas kernels, layer(): pl.pallas_call(layer_kernel, out_shape=jax.ShapeDtypeStruct((2, 32, COLS)...  120 us

profile of v6, /device:TPU:1, one launch (start us, length us, event | category | flops | bytes accessed | tf_op | source)
XLA Modules:
  0.0 121.1 jit_solution(6976013872840750514)
XLA Ops:
  0.0 119.6 %shard_map.136 = bf16[2,32,448]{2,1,0:T(8,128)(2,1)} custom-call(bf16[2,32,16,576]{3,2,1,0:T(8,128)(2,1)} %queries.1, bf16[2,32,576]{2,1,0:T(8,128)(2,1)} %fresh_hbm.1, bf16[576,20480]{1,0:T(8,128)(2,1)} %bitcast.8, s32[10,32]{1,0:T(8,128)} %bitcast.12, s32[1,256]{1,0:T(1,128)} %bitcast.13, s32[1,16]{1,0:T(1,128)} %bitcast.15, s32[1,256]{1,0:T(1,128)} %bitcast.14, ...), custom_call_target="tpu_custom_call" | custom-call | tf_op jit(solution)/shard_map/pallas_call | solution.py:586
  119.6 1.5 %copy.16 = bf16[2,32,448]{2,1,0:T(8,128)(2,1)} copy(bf16[2,32,448]{2,1,0:T(8,128)(2,1)} %shard_map.136) | data formatting | bytes 114688
